TPU v7x, 512 devices: a whole 4x8x8 slice. The times are simulated.
512 devices in a mesh: item: 8 (over z), seq: 64 (over x, y, core).
Axes of the slice: x: 4, y: 8, z: 8, core: 2. Of those that a mesh axis runs over, the one named last changes fastest.
Arguments:
- item_states: bfloat16 [16384, 2048], P(('item', 'seq')), may hold values from -6 to 6
- item_gain: float32 [2048], replicated, may hold values from 0.25 to 1.75
- hist_ids: int32 [32768], P('seq'), may hold values from 0 to 16383, as said below
- lengths: int32 [8], replicated, may hold values from 1 to 4096, as said below
- attn_gain: float32 [2048], replicated, may hold values from 0.25 to 1.75
- w_q: bfloat16 [2048, 2048], P(None, 'item')
- w_kv: bfloat16 [2048, 2, 1024], P(None, None, 'item')
- q_gain: float32 [128], replicated
- k_gain: float32 [128], replicated
- w_out: bfloat16 [2048, 2048], P('item'), may hold values from -0.125 to 0.125
Outputs:
- mixed: bfloat16 [32768, 2048], P('seq', 'item')
Inputs may be any that keep to these rules, and one draw needn't show every extreme that they name: `hist_ids`: among the 512 slots of one index of seq, at most 2 refer to items of one block of 32 consecutive ids, and in every such group of slots some block has exactly 2. `lengths`: some user has the full 4096 slots.
All inputs are finite; a program needn't handle non-finite values.
Results may differ from a plain program's by a relative error of at most 0.014.
Values may be sent and summed in bfloat16 or wider, within the bound.
A program may use at most 64 MiB of HBM per device.

v0:
```python
import jax
import jax.numpy as jnp
from jax import lax
from jax.sharding import PartitionSpec as P

HD = 128
LEN = 4096


def from_behind(value, axis, steps):
    count = lax.axis_size(axis)
    first, last = (max(0, -steps), min(count, count - steps))
    return lax.ppermute(value, axis, [(source, source + steps) for source in range(first, last)])


def rms(x, gain):
    return x * lax.rsqrt(jnp.mean(x * x, axis=-1, keepdims=True) + 1e-06) * gain


def body(item_states, item_gain, hist_ids, lengths, attn_gain, w_q, w_kv, q_gain, k_gain, w_out):
    n_seq = lax.axis_size("seq")
    n_item = lax.axis_size("item")
    my_item = lax.axis_index("item")
    my_seq = lax.axis_index("seq")
    per_dev = item_states.shape[0]
    width = item_states.shape[1]
    rows = hist_ids.shape[0]
    capacity = max(2, 2 * rows // (n_item * n_seq))
    embed = rms(item_states.astype(jnp.float32), item_gain).astype(jnp.bfloat16)
    owner = hist_ids // per_dev
    owner_row = owner // n_seq
    owner_col = owner % n_seq
    slot_iota = jnp.arange(rows, dtype=jnp.int32)
    before = (owner[:, None] == owner[None, :]) & (slot_iota[:, None] > slot_iota[None, :])
    rank = jnp.sum(before.astype(jnp.int32), axis=1)
    mine = owner_row == my_item
    target = jnp.where(mine, owner_col * capacity + rank, n_seq * capacity)
    wanted = (
        jnp.zeros((n_seq * capacity,), jnp.int32).at[target].set(hist_ids % per_dev, mode="drop")
    )
    wanted = wanted.reshape(n_seq, capacity)
    table_iota = jnp.arange(per_dev, dtype=jnp.int32)
    onehot = (
        lax.all_to_all(wanted, "seq", split_axis=0, concat_axis=0, tiled=True)[..., None]
        == table_iota
    ).astype(jnp.bfloat16)
    found = jnp.einsum("scn,nd->scd", onehot, embed, preferred_element_type=jnp.float32).astype(
        jnp.bfloat16
    )
    fetched = lax.all_to_all(found, "seq", split_axis=0, concat_axis=0, tiled=True)
    every = lax.all_gather(fetched, "item", axis=0, tiled=True).reshape(-1, width)
    hist = jnp.take(every, owner * capacity + rank, axis=0)
    normed = rms(hist.astype(jnp.float32), attn_gain).astype(jnp.bfloat16)
    kv_local = w_kv.shape[2] // HD
    group = w_q.shape[1] // HD // kv_local
    query = jnp.dot(normed, w_q, preferred_element_type=jnp.float32).reshape(
        rows, kv_local, group, HD
    )
    query = rms(query, q_gain).astype(jnp.bfloat16)
    pairs = jnp.einsum("rd,dtc->trc", normed, w_kv, preferred_element_type=jnp.float32)
    pairs = pairs.reshape(2, rows, kv_local, HD)
    key_half = rms(pairs[0], k_gain).astype(jnp.bfloat16)
    value_half = pairs[1].astype(jnp.bfloat16)
    kv_pair = jnp.stack([key_half, value_half], axis=0)
    span = LEN // rows
    slot_pos = my_seq % span
    base = slot_pos * rows
    user = my_seq * rows // LEN
    length = lengths[user]
    query_pos = base + slot_iota
    scale = 1.0 / HD**0.5

    def absorb(state, pair, key_base):
        top, total, acc = state
        key_pos = key_base + slot_iota
        allowed = (
            (key_pos[None, :] <= query_pos[:, None])
            & (key_pos[None, :] < length)
            & (key_pos[None, :] >= 0)
        )
        score = (
            jnp.einsum("rkgc,skc->kgrs", query, pair[0], preferred_element_type=jnp.float32) * scale
        )
        score = jnp.where(allowed, score, -1e30)
        new_top = jnp.maximum(top, jnp.max(score, axis=-1))
        weights = jnp.where(allowed, jnp.exp(score - new_top[..., None]), 0.0)
        shrink = jnp.exp(top - new_top)
        total = total * shrink + jnp.sum(weights, axis=-1)
        acc = acc * shrink[..., None] + jnp.einsum(
            "kgrs,skc->kgrc",
            weights.astype(jnp.bfloat16),
            pair[1],
            preferred_element_type=jnp.float32,
        )
        return (new_top, total, acc)

    start_state = (
        jnp.full((kv_local, group, rows), -1e30, jnp.float32),
        jnp.zeros((kv_local, group, rows), jnp.float32),
        jnp.zeros((kv_local, group, rows, HD), jnp.float32),
    )
    state = absorb(start_state, kv_pair, base)

    def cycle_step(step, carry):
        pair, state = carry
        pair = from_behind(pair, "seq", 1)
        key_base = base - step * rows
        state = absorb(state, pair, key_base)
        return (pair, state)

    kv_pair, state = lax.fori_loop(1, span, cycle_step, (kv_pair, state))
    top, total, acc = state
    attn = (acc / total[..., None]).astype(jnp.bfloat16)
    attn = jnp.transpose(attn, (2, 0, 1, 3)).reshape(rows, kv_local * group * HD)
    proj = jnp.dot(attn, w_out, preferred_element_type=jnp.float32)
    proj = jnp.where((query_pos < length)[:, None], proj, 0.0)
    share = lax.psum_scatter(
        proj.astype(jnp.bfloat16), "item", scatter_dimension=1, tiled=True
    ).astype(jnp.float32)
    cols = width // n_item
    residual = lax.dynamic_slice_in_dim(hist, my_item * cols, cols, 1).astype(jnp.float32)
    return (residual + share).astype(jnp.bfloat16)


def solution(mesh):
    placed = (
        P(("item", "seq"), None),
        P(),
        P("seq"),
        P(),
        P(),
        P(None, "item"),
        P(None, None, "item"),
        P(),
        P(),
        P("item", None),
    )
    return jax.shard_map(
        body, mesh=mesh, in_specs=placed, out_specs=P("seq", "item"), check_vma=False
    )
```

profile of v0, /device:TPU:56, one launch (start us, length us, event | category | flops | bytes accessed | tf_op | source)
XLA Modules:
  0.0 267.7 jit_solution(6962511304838909033)
XLA Ops:
  7.7 2.4 scatter_custom_fusion
  10.9 9.9 %all-to-all-start = ((s32[64,1,2]{2,1,0:T(1,128)}), s32[64,1,2]{2,1,0:T(1,128)S(1)}, u32[]{:S(2)}, u32[]{:S(2)}) async-start(s32[64,1,2]{2,1,0:T(1,128)} %bitcast), calls=%async_computation | async-start | bytes 65536 | tf_op jit(solution)/shard_map/all_to_all | solution.py:44
  21.8 6.2 %all-to-all-done = s32[64,1,2]{2,1,0:T(1,128)S(1)} async-done(((s32[64,1,2]{2,1,0:T(1,128)}), s32[64,1,2]{2,1,0:T(1,128)S(1)}, u32[]{:S(2)}, u32[]{:S(2)}) %all-to-all-start) | async-done | bytes 544 | tf_op jit(solution)/shard_map/all_to_all | solution.py:44
  28.1 1.3 convolution_convert_fusion
  29.9 22.6 %all_to_all.14 = bf16[64,2,2048]{2,1,0:T(2,128)(2,1)} all-to-all(bf16[64,2,2048]{2,1,0:T(2,128)(2,1)S(1)} %copy.58), channel_id=1, replica_groups=mesh['item'=8,'seq'=64] {'seq'}, dimensions={0} | all-to-all | bytes 1048576 | tf_op jit(solution)/shard_map/all_to_all | solution.py:50
  52.9 2.1 copy.59
  56.6 56.2 %all-gather.2.cloned.1.call-done = bf16[512,2,2048]{2,1,0:T(2,128)(2,1)} async-done(((bf16[64,2,2048]{2,1,0:T(2,128)(2,1)}), bf16[512,2,2048]{2,1,0:T(2,128)(2,1)}) %all-gather.2.cloned.1.call-update) | async-done | bytes 4194320 | tf_op jit(solution)/shard_map/all_gather | solution.py:51
  112.8 7.2 %reshape.408 = bf16[1024,2048]{1,0:T(8,128)(2,1)} reshape(bf16[512,2,2048]{2,1,0:T(2,128)(2,1)} %all-gather.2.cloned.1.call-done) | data formatting | bytes 8388608 | tf_op jit(solution)/shard_map/reshape | solution.py:51
  120.0 7.1 %gather_fusion = bf16[512,2048]{1,0:T(8,128)(2,1)S(1)} fusion(bf16[1024,2048]{1,0:T(8,128)(2,1)} %reshape.408, s32[1024]{0:T(1024)S(1)} %pad_clamp_fusion), kind=kCustom, calls=%fused_computation | custom fusion | bytes 4196352 | tf_op jit(solution)/shard_map/jit(_take)/gather | solution.py:52
  134.2 73.8 %while.21 = (s32[]{:T(128)}, bf16[2,512,1,128]{3,1,2,0:T(8,128)(2,1)S(1)}, f32[1,2,512]{2,1,0:T(2,128)S(1)}, f32[1,2,512]{2,1,0:T(2,128)S(1)}, f32[1,2,512,128]{...) while((s32[]{:T(128)}, ...), condition=%wide.region_11.12_spmd.clone.clone, body=%wide.region_8.11_spmd.clone.clone.sunk | while | flops 276305408 | bytes 10561717 | solution.py:111
  134.2 1.9 collective-permute-start
  137.2 4.8 %collective-permute-done = bf16[2,512,1,128]{3,1,2,0:T(8,128)(2,1)S(1)} collective-permute-done((bf16[2,512,1,128]{3,1,2,0:T(8,128)(2,1)S(1)}, bf16[2,512,1,128]{3,1,2,0:T(8,128)(2,1)S(1)}, u32[]{:S(2)}, u32[]{:S(2)}) %collective-permute-start) | collective-permute-done | bytes 262176 | tf_op jit(solution)/shard_map/while/body/eval_jaxpr/ppermute | solution.py:13
  144.1 1.9 collective-permute-start
  147.0 4.8 %collective-permute-done = bf16[2,512,1,128]{3,1,2,0:T(8,128)(2,1)S(1)} collective-permute-done((bf16[2,512,1,128]{3,1,2,0:T(8,128)(2,1)S(1)}, bf16[2,512,1,128]{3,1,2,0:T(8,128)(2,1)S(1)}, u32[]{:S(2)}, u32[]{:S(2)}) %collective-permute-start) | collective-permute-done | bytes 262176 | tf_op jit(solution)/shard_map/while/body/eval_jaxpr/ppermute | solution.py:13
  153.9 3.0 %collective-permute-start = (bf16[2,512,1,128]{3,1,2,0:T(8,128)(2,1)S(1)}, bf16[2,512,1,128]{3,1,2,0:T(8,128)(2,1)S(1)}, u32[]{:S(2)}, u32[]{:S(2)}) collective-permute-start(bf16[2,512,1,128]{3,1,2,0:T(8,128)(2,1)S(1)} %get-tuple-element.373), channel_id=1, source_target_pairs={{0,1},{1,2},{2,3},{3,4},{4,5},{5,6},{6,7},{7,8},{8,9},{9,10},{10,1... | collective-permute-start | bytes 786440 | tf_op jit(solution)/shard_map/while/body/eval_jaxpr/ppermute | solution.py:13
  157.9 3.7 %collective-permute-done = bf16[2,512,1,128]{3,1,2,0:T(8,128)(2,1)S(1)} collective-permute-done((bf16[2,512,1,128]{3,1,2,0:T(8,128)(2,1)S(1)}, bf16[2,512,1,128]{3,1,2,0:T(8,128)(2,1)S(1)}, u32[]{:S(2)}, u32[]{:S(2)}) %collective-permute-start) | collective-permute-done | bytes 262176 | tf_op jit(solution)/shard_map/while/body/eval_jaxpr/ppermute | solution.py:13
  163.8 5.1 %collective-permute-start = (bf16[2,512,1,128]{3,1,2,0:T(8,128)(2,1)S(1)}, bf16[2,512,1,128]{3,1,2,0:T(8,128)(2,1)S(1)}, u32[]{:S(2)}, u32[]{:S(2)}) collective-permute-start(bf16[2,512,1,128]{3,1,2,0:T(8,128)(2,1)S(1)} %get-tuple-element.373), channel_id=1, source_target_pairs={{0,1},{1,2},{2,3},{3,4},{4,5},{5,6},{6,7},{7,8},{8,9},{9,10},{10,1... | collective-permute-start | bytes 786440 | tf_op jit(solution)/shard_map/while/body/eval_jaxpr/ppermute | solution.py:13
  169.9 1.6 collective-permute-done
  173.6 7.2 %collective-permute-start = (bf16[2,512,1,128]{3,1,2,0:T(8,128)(2,1)S(1)}, bf16[2,512,1,128]{3,1,2,0:T(8,128)(2,1)S(1)}, u32[]{:S(2)}, u32[]{:S(2)}) collective-permute-start(bf16[2,512,1,128]{3,1,2,0:T(8,128)(2,1)S(1)} %get-tuple-element.373), channel_id=1, source_target_pairs={{0,1},{1,2},{2,3},{3,4},{4,5},{5,6},{6,7},{7,8},{8,9},{9,10},{10,1... | collective-permute-start | bytes 786440 | tf_op jit(solution)/shard_map/while/body/eval_jaxpr/ppermute | solution.py:13
  184.1 8.7 %collective-permute-start = (bf16[2,512,1,128]{3,1,2,0:T(8,128)(2,1)S(1)}, bf16[2,512,1,128]{3,1,2,0:T(8,128)(2,1)S(1)}, u32[]{:S(2)}, u32[]{:S(2)}) collective-permute-start(bf16[2,512,1,128]{3,1,2,0:T(8,128)(2,1)S(1)} %get-tuple-element.373), channel_id=1, source_target_pairs={{0,1},{1,2},{2,3},{3,4},{4,5},{5,6},{6,7},{7,8},{8,9},{9,10},{10,1... | collective-permute-start | bytes 786440 | tf_op jit(solution)/shard_map/while/body/eval_jaxpr/ppermute | solution.py:13
  196.1 8.7 %collective-permute-start = (bf16[2,512,1,128]{3,1,2,0:T(8,128)(2,1)S(1)}, bf16[2,512,1,128]{3,1,2,0:T(8,128)(2,1)S(1)}, u32[]{:S(2)}, u32[]{:S(2)}) collective-permute-start(bf16[2,512,1,128]{3,1,2,0:T(8,128)(2,1)S(1)} %get-tuple-element.373), channel_id=1, source_target_pairs={{0,1},{1,2},{2,3},{3,4},{4,5},{5,6},{6,7},{7,8},{8,9},{9,10},{10,1... | collective-permute-start | bytes 786440 | tf_op jit(solution)/shard_map/while/body/eval_jaxpr/ppermute | solution.py:13
  208.3 2.0 select_convert_fusion
  210.4 48.7 %reduce-scatter.2.cloned.1.call-done = bf16[512,256]{1,0:T(8,128)(2,1)} async-done(((bf16[512,2048]{1,0:T(8,128)(2,1)}), bf16[512,256]{1,0:T(8,128)(2,1)}) %reduce-scatter.2.cloned.1.call-update) | async-done | bytes 262160 | tf_op jit(solution)/shard_map/reduce_scatter | solution.py:117
  259.1 1.8 add_convert_fusion
  (132 shorter events, 34.6 us)
Async XLA Ops:
  6.5 201.8 %copy-start = (bf16[256,2048]{1,0:T(8,128)(2,1)S(1)}, bf16[256,2048]{1,0:T(8,128)(2,1)}, u32[]{:S(2)}) copy-start(bf16[256,2048]{1,0:T(8,128)(2,1)} %param.21) | copy-start | bytes 3145732
  6.5 46.3 %copy-start.2 = (bf16[2048,2,128]{2,1,0:T(2,128)(2,1)S(1)}, bf16[2048,2,128]{2,1,0:T(2,128)(2,1)}, u32[]{:S(2)}) copy-start(bf16[2048,2,128]{2,1,0:T(2,128)(2,1)} %param.18) | copy-start | bytes 3145732
  10.9 17.2 %all-to-all-start = ((s32[64,1,2]{2,1,0:T(1,128)}), s32[64,1,2]{2,1,0:T(1,128)S(1)}, u32[]{:S(2)}, u32[]{:S(2)}) async-start(s32[64,1,2]{2,1,0:T(1,128)} %bitcast), calls=%async_computation | async-start | bytes 65536 | tf_op jit(solution)/shard_map/all_to_all | solution.py:44
  20.8 92.0 %all-gather.2.cloned.1.call-start = ((), (), s32[]{:S(2)}) async-start(), calls=%async_computation.3 | async-start | bytes 4718592 | tf_op jit(solution)/shard_map/all_gather | solution.py:51
  29.9 25.0 %copy-start.8 = (s32[8]{0:T(128)S(1)}, s32[8]{0:T(128)}, u32[]{:S(2)}) copy-start(s32[8]{0:T(128)} %param.15) | copy-start | bytes 100
  29.9 26.4 %copy-start.5 = (f32[128]{0:T(128)S(1)}, f32[128]{0:T(128)}, u32[]{:S(2)}) copy-start(f32[128]{0:T(128)} %param.19) | copy-start | bytes 1540
  52.6 206.5 %reduce-scatter.2.cloned.1.call-start = ((), (), s32[]{:S(2)}) async-start(), calls=%async_computation.4 | async-start | bytes 2359296 | tf_op jit(solution)/shard_map/reduce_scatter | solution.py:117
  127.1 1.2 copy-start.3
  127.1 1.2 copy-start.7
  127.9 1.4 copy-start.1
  128.3 1.5 copy-start.6
  130.8 0.7 copy-start.4
  134.2 7.7 %collective-permute-start = (bf16[2,512,1,128]{3,1,2,0:T(8,128)(2,1)S(1)}, bf16[2,512,1,128]{3,1,2,0:T(8,128)(2,1)S(1)}, u32[]{:S(2)}, u32[]{:S(2)}) collective-permute-start(bf16[2,512,1,128]{3,1,2,0:T(8,128)(2,1)S(1)} %get-tuple-element.373), channel_id=1, source_target_pairs={{0,1},{1,2},{2,3},{3,4},{4,5},{5,6},{6,7},{7,8},{8,9},{9,10},{10,1... | collective-permute-start | bytes 786440 | tf_op jit(solution)/shard_map/while/body/eval_jaxpr/ppermute | solution.py:13
  144.1 7.7 %collective-permute-start = (bf16[2,512,1,128]{3,1,2,0:T(8,128)(2,1)S(1)}, bf16[2,512,1,128]{3,1,2,0:T(8,128)(2,1)S(1)}, u32[]{:S(2)}, u32[]{:S(2)}) collective-permute-start(bf16[2,512,1,128]{3,1,2,0:T(8,128)(2,1)S(1)} %get-tuple-element.373), channel_id=1, source_target_pairs={{0,1},{1,2},{2,3},{3,4},{4,5},{5,6},{6,7},{7,8},{8,9},{9,10},{10,1... | collective-permute-start | bytes 786440 | tf_op jit(solution)/shard_map/while/body/eval_jaxpr/ppermute | solution.py:13
  153.9 7.7 %collective-permute-start = (bf16[2,512,1,128]{3,1,2,0:T(8,128)(2,1)S(1)}, bf16[2,512,1,128]{3,1,2,0:T(8,128)(2,1)S(1)}, u32[]{:S(2)}, u32[]{:S(2)}) collective-permute-start(bf16[2,512,1,128]{3,1,2,0:T(8,128)(2,1)S(1)} %get-tuple-element.373), channel_id=1, source_target_pairs={{0,1},{1,2},{2,3},{3,4},{4,5},{5,6},{6,7},{7,8},{8,9},{9,10},{10,1... | collective-permute-start | bytes 786440 | tf_op jit(solution)/shard_map/while/body/eval_jaxpr/ppermute | solution.py:13
  163.8 7.7 %collective-permute-start = (bf16[2,512,1,128]{3,1,2,0:T(8,128)(2,1)S(1)}, bf16[2,512,1,128]{3,1,2,0:T(8,128)(2,1)S(1)}, u32[]{:S(2)}, u32[]{:S(2)}) collective-permute-start(bf16[2,512,1,128]{3,1,2,0:T(8,128)(2,1)S(1)} %get-tuple-element.373), channel_id=1, source_target_pairs={{0,1},{1,2},{2,3},{3,4},{4,5},{5,6},{6,7},{7,8},{8,9},{9,10},{10,1... | collective-permute-start | bytes 786440 | tf_op jit(solution)/shard_map/while/body/eval_jaxpr/ppermute | solution.py:13
  173.6 8.3 %collective-permute-start = (bf16[2,512,1,128]{3,1,2,0:T(8,128)(2,1)S(1)}, bf16[2,512,1,128]{3,1,2,0:T(8,128)(2,1)S(1)}, u32[]{:S(2)}, u32[]{:S(2)}) collective-permute-start(bf16[2,512,1,128]{3,1,2,0:T(8,128)(2,1)S(1)} %get-tuple-element.373), channel_id=1, source_target_pairs={{0,1},{1,2},{2,3},{3,4},{4,5},{5,6},{6,7},{7,8},{8,9},{9,10},{10,1... | collective-permute-start | bytes 786440 | tf_op jit(solution)/shard_map/while/body/eval_jaxpr/ppermute | solution.py:13
  184.1 9.8 %collective-permute-start = (bf16[2,512,1,128]{3,1,2,0:T(8,128)(2,1)S(1)}, bf16[2,512,1,128]{3,1,2,0:T(8,128)(2,1)S(1)}, u32[]{:S(2)}, u32[]{:S(2)}) collective-permute-start(bf16[2,512,1,128]{3,1,2,0:T(8,128)(2,1)S(1)} %get-tuple-element.373), channel_id=1, source_target_pairs={{0,1},{1,2},{2,3},{3,4},{4,5},{5,6},{6,7},{7,8},{8,9},{9,10},{10,1... | collective-permute-start | bytes 786440 | tf_op jit(solution)/shard_map/while/body/eval_jaxpr/ppermute | solution.py:13
  196.1 9.8 %collective-permute-start = (bf16[2,512,1,128]{3,1,2,0:T(8,128)(2,1)S(1)}, bf16[2,512,1,128]{3,1,2,0:T(8,128)(2,1)S(1)}, u32[]{:S(2)}, u32[]{:S(2)}) collective-permute-start(bf16[2,512,1,128]{3,1,2,0:T(8,128)(2,1)S(1)} %get-tuple-element.373), channel_id=1, source_target_pairs={{0,1},{1,2},{2,3},{3,4},{4,5},{5,6},{6,7},{7,8},{8,9},{9,10},{10,1... | collective-permute-start | bytes 786440 | tf_op jit(solution)/shard_map/while/body/eval_jaxpr/ppermute | solution.py:13
Sparse Core Ops, SparseCore 0:
  52.7 60.0 all-gather.1
  210.5 48.5 reduce-scatter.1
where the time goes:
time: 269 us; the launch traced here: 268 us
  waiting for transfers between devices  126 us (47%)
  starting transfers between devices  46.5 us (17%)
  local copies, waits for them, and re-layouts  22.9 us (9%)
  blocking collectives  22.6 us (8%)
  other arithmetic  17.8 us (7%)
  matrix products  17.1 us (6%)
  between operations  13.8 us (5%)
    all_gather x1, waiting for transfers between devices, body(): lax.all_gather(fetched, 'item', axis=0, tiled=True).reshape(-1, width)  56.2 us
    reduce_scatter x1, waiting for transfers between devices, body(): lax.psum_scatter(proj.astype(jnp.bfloat16), 'item', scatter_dimension=1,...  48.7 us
    ppermute x7, starting transfers between devices, from_behind(): lax.ppermute(value, axis, [(source, source + steps) for source in range(f...  36.4 us
    all_to_all x1, blocking collectives, body(): lax.all_to_all(found, 'seq', split_axis=0, concat_axis=0, tiled=True)  22.6 us
    ppermute x7, waiting for transfers between devices, from_behind(): lax.ppermute(value, axis, [(source, source + steps) for source in range(f...  15.3 us
    all_to_all x1, starting transfers between devices, body(): lax.all_to_all(wanted, 'seq', split_axis=0, concat_axis=0, tiled=True)  9.89 us
    dot_general x8, matrix products, absorb(): jnp.einsum('kgrs,skc->kgrc', weights.astype(jnp.bfloat16), pair[1], prefe...  7.53 us
    reshape x1, local copies, waits for them, and re-layouts, body(): lax.all_gather(fetched, 'item', axis=0, tiled=True).reshape(-1, width)  7.2 us
  transfers between devices with their start and end apart: 10, of which 10 were waited for; matrix products, arithmetic and copies ran while one was open for 4% of the time, Pallas kernels for 0%

commit v1 on v0

v1 whole, which is shorter than its diff:
```python
import functools

import jax
import jax.numpy as jnp
from jax import lax
from jax.experimental import pallas as pl
from jax.experimental.pallas import tpu as pltpu
from jax.sharding import PartitionSpec as P

HD = 128
LEN = 4096
CORES = 2
NY = 8
F32, BF16, I32 = jnp.float32, jnp.bfloat16, jnp.int32
VMEM_LIMIT = 48 * 1024 * 1024


def rms(x, gain):
    return x * lax.rsqrt(jnp.mean(x * x, axis=-1, keepdims=True) + 1e-06) * gain


def iota(shape, dim):
    return lax.broadcasted_iota(I32, shape, dim)


def onehot(mask):
    return jnp.where(mask, 1.0, 0.0).astype(BF16)


def dot(a, b):
    return jnp.dot(a, b, preferred_element_type=F32)


def signal(sem, **where):
    pl.semaphore_signal(sem, inc=1, device_id=where, device_id_type=pl.DeviceIdType.MESH)


def remote(src, dst, send, recv, **where):
    return pltpu.make_async_remote_copy(
        src_ref=src, dst_ref=dst, send_sem=send, recv_sem=recv,
        device_id=where, device_id_type=pl.DeviceIdType.MESH,
    )


class ZRing:
    def __init__(self, buf, send, recv, n):
        self.buf, self.send, self.recv, self.n = buf, send, recv, n
        self.me = lax.axis_index("item")

    def live(self, way, hop, half):
        return hop < self.n // 2 or (hop == self.n // 2 and half == way)

    def copy(self, way, hop, half, shard):
        step = 1 if way == 0 else self.n - 1
        piece = self.buf.at[shard * 2 + half]
        at = (way, hop - 1, half)
        return remote(
            piece, piece, self.send.at[at], self.recv.at[at],
            item=lax.rem(self.me + step, self.n),
        )

    def shard(self, way, hop):
        return lax.rem(self.me + (self.n - hop if way == 0 else hop), self.n)

    def start(self, hop):
        for half in range(2):
            self.start_half(hop, half)

    def start_half(self, hop, half):
        for way in range(2):
            if self.live(way, hop, half):
                self.copy(way, hop, half, self.shard(way, hop - 1)).start()

    def land(self, hop):
        for half in range(2):
            for way in range(2):
                if self.live(way, hop, half):
                    self.copy(way, hop, half, self.shard(way, hop)).wait_recv()
                    if self.live(way, hop + 1, half):
                        self.copy(way, hop + 1, half, self.shard(way, hop)).start()

    def drain(self):
        for hop in range(1, self.n // 2 + 1):
            for half in range(2):
                for way in range(2):
                    if self.live(way, hop, half):
                        self.copy(way, hop, half, self.shard(way, hop - 1)).wait_send()


def rank_of(ids_row, ids_col, per_dev, n_seq, axis):
    rows = ids_row.shape[1]
    owner_row = (ids_row // per_dev) & (n_seq - 1)
    owner_col = (ids_col // per_dev) & (n_seq - 1)
    lane, sub = iota((rows, rows), 1), iota((rows, rows), 0)
    if axis == 0:
        same = (owner_col == owner_row) & (sub < lane)
        less = owner_col < owner_row
    else:
        same = (owner_col == owner_row) & (lane < sub)
        less = owner_row < owner_col
    within = jnp.sum(jnp.where(same, 1.0, 0.0), axis=axis, keepdims=True).astype(I32)
    before = jnp.sum(jnp.where(less, 1.0, 0.0), axis=axis, keepdims=True).astype(I32)
    return before + within, within


def fetch_kernel(
    n_item, n_seq, ny, ids_row_ref, ids_col_ref, states_ref, gain_ref, out_ref,
    table, id_a, id_b, id_c, id_d, found, mid, turned, final,
    z_send, z_recv, iy_send, iy_recv, ix_send, ix_recv, rx_send, rx_recv, ry_send, ry_recv,
):
    nq = n_seq // ny
    me = lax.axis_index("item")
    my_seq = lax.axis_index("seq")
    my_core = lax.rem(my_seq, CORES)
    my_y = lax.rem(my_seq // CORES, ny)
    my_x = my_seq // (CORES * ny)
    my_q = my_x * CORES + my_core
    per_dev, width = states_ref.shape
    rows = ids_row_ref.shape[1]
    share = rows // n_item

    def along_y(y):
        return (my_x * ny + y) * CORES + my_core

    def along_q(q):
        return ((q // CORES) * ny + my_y) * CORES + lax.rem(q, CORES)

    def y_plus(d):
        return lax.rem(my_y + d, ny)

    def q_plus(d):
        return lax.rem(my_q + d, nq)

    barrier = pltpu.get_barrier_semaphore()
    for step in (1, n_item - 1):
        signal(barrier, item=lax.rem(me + step, n_item))
    for d in range(1, ny):
        signal(barrier, seq=along_y(y_plus(d)))
    for d in range(1, nq):
        signal(barrier, seq=along_q(q_plus(d)))

    embed = rms(states_ref[...].astype(F32), gain_ref[...]).astype(BF16)
    half = per_dev // 2
    table[pl.ds(me * 2, 2)] = embed.reshape(2, half, width)
    pl.semaphore_wait(barrier, 2 + (ny - 1) + (nq - 1))

    ring = ZRing(table, z_send, z_recv, n_item)
    ring.start(1)

    ids_row = ids_row_ref[...]
    rank, within = rank_of(ids_row, ids_col_ref[...], per_dev, n_seq, 0)
    owner = ids_row // per_dev
    owner_seq = owner & (n_seq - 1)
    source_y = (owner_seq // CORES) & (ny - 1)
    source_q = (owner_seq // (CORES * ny)) * CORES + (owner_seq & (CORES - 1))
    item = (owner // n_seq) * per_dev + (ids_row & (per_dev - 1)) + 1
    mine = (rank & (n_item - 1)) == me
    copy_no = within // n_item
    place = jnp.where(mine, source_y * nq + source_q, -1)
    asked = []
    for sub in range(2):
        hit = (iota((ny * nq, rows), 0) == place) & (copy_no == sub)
        asked.append(jnp.sum(jnp.where(hit, item.astype(F32), 0.0), axis=1, keepdims=True).astype(I32))
    lanes = iota((ny * nq, 128), 1)
    id_a[...] = jnp.where(lanes == 0, asked[0], jnp.where(lanes == 1, asked[1], 0)).reshape(ny, nq, 128)

    def ids_y(d, y_from, y_to):
        return remote(
            id_a.at[y_to], id_b.at[y_from], iy_send.at[d - 1], iy_recv.at[d - 1], seq=along_y(y_to)
        )

    def ids_q(d, q_from, q_to):
        return remote(
            id_c.at[q_to], id_d.at[q_from], ix_send.at[d - 1], ix_recv.at[d - 1], seq=along_q(q_to)
        )

    for d in range(1, ny):
        ids_y(d, my_y, y_plus(d)).start()
    id_b[my_y] = id_a[my_y]
    ring.land(1)
    for d in range(1, ny):
        ids_y(d, y_plus(ny - d), my_y).wait_recv()
    for q in range(nq):
        id_c[q] = id_b[:, q, :]
    for d in range(1, nq):
        ids_q(d, my_q, q_plus(d)).start()
    id_d[my_q] = id_c[my_q]
    for hop in range(2, n_item // 2):
        ring.land(hop)
    spot = jnp.where(mine, rank // n_item, -1)
    pick_a = onehot(iota((share, rows), 0) == spot)
    pick_b = onehot(iota((ny * nq * 2, rows), 0) == jnp.where(mine, place * 2 + copy_no, -1))
    pick = lax.dot_general(pick_a, pick_b, (((1,), (1,)), ((), ())), preferred_element_type=F32).astype(BF16)
    for d in range(1, nq):
        ids_q(d, q_plus(nq - d), my_q).wait_recv()
    wanted = id_d[...].reshape(nq * ny, 128)
    items = iota((nq * ny, n_item * per_dev), 1) + 1
    choose = jnp.stack(
        [jnp.where(wanted[:, sub:sub + 1] == items, 1.0, 0.0).reshape(nq, ny, n_item * per_dev) for sub in range(2)],
        axis=1,
    ).reshape(nq * 2 * ny, n_item * per_dev).astype(BF16)
    if n_item > 2:
        ring.land(n_item // 2)
    else:
        pass

    parts = found.shape[0]
    cols = width // parts
    to, frm = iota((ny * nq * 2, nq * 2 * ny), 0), iota((ny * nq * 2, nq * 2 * ny), 1)
    to_y, to_q, to_sub = to // (nq * 2), (to // 2) % nq, to % 2
    turn = onehot(frm == (to_q * 2 + to_sub) * ny + to_y)

    def rows_q(part, d, q_from, q_to):
        return remote(
            found.at[part, q_to], mid.at[part, q_from],
            rx_send.at[part, d - 1], rx_recv.at[part, d - 1], seq=along_q(q_to),
        )

    def rows_y(part, d, y_from, y_to):
        return remote(
            turned.at[part, y_to], final.at[part, y_from],
            ry_send.at[part, d - 1], ry_recv.at[part, d - 1], seq=along_y(y_to),
        )

    for part in range(parts):
        span = slice(part * cols, (part + 1) * cols)
        source = table[:, :, span].reshape(n_item * per_dev, cols)
        found[part] = dot(choose, source).astype(BF16).reshape(nq, 2 * ny, cols)
        for d in range(1, nq):
            rows_q(part, d, my_q, q_plus(d)).start()
        mid[part, my_q] = found[part, my_q]
    for part in range(parts):
        for d in range(1, nq):
            rows_q(part, d, q_plus(nq - d), my_q).wait_recv()
        turned[part] = dot(turn, mid[part].reshape(nq * 2 * ny, cols)).astype(BF16).reshape(ny, 2 * nq, cols)
        for d in range(1, ny):
            rows_y(part, d, my_y, y_plus(d)).start()
        final[part, my_y] = turned[part, my_y]
    for part in range(parts):
        for d in range(1, ny):
            rows_y(part, d, y_plus(ny - d), my_y).wait_recv()
        out_ref[:, part * cols:(part + 1) * cols] = dot(
            pick, final[part].reshape(ny * 2 * nq, cols)
        ).astype(BF16)

    ring.drain()
    for d in range(1, ny):
        ids_y(d, my_y, y_plus(d)).wait_send()
    for d in range(1, nq):
        ids_q(d, my_q, q_plus(d)).wait_send()
    for part in range(parts):
        for d in range(1, nq):
            rows_q(part, d, my_q, q_plus(d)).wait_send()
        for d in range(1, ny):
            rows_y(part, d, my_y, y_plus(d)).wait_send()


def attend_kernel(
    n_item, n_seq, per_dev, ids_row_ref, ids_col_ref, len_ref, rows_ref, again_ref, wq_ref, wkv_ref,
    qg_ref, kg_ref, attn_ref, res_ref,
    every, ranked, query, kv, acc, top, total,
    z_send, z_recv, lane_send, lane_recv, pair_send, pair_recv,
):
    me = lax.axis_index("item")
    my_seq = lax.axis_index("seq")
    rows = ids_row_ref.shape[1]
    share, width = rows_ref.shape
    span = LEN // rows
    chips = span // CORES
    core = lax.rem(my_seq, CORES)
    chip = lax.rem(my_seq // CORES, chips)
    other = 1 - core
    base = lax.rem(my_seq, span) * rows
    length = len_ref[my_seq // span]
    q_cols = wq_ref.shape[1]
    group = q_cols // HD
    cols = width // n_item
    sibling = my_seq + 1 - 2 * core

    barrier = pltpu.get_barrier_semaphore()
    for step in (1, n_item - 1):
        signal(barrier, item=lax.rem(me + step, n_item))
    signal(barrier, seq=sibling)

    @pl.when(chip > 0)
    def _():
        signal(barrier, seq=my_seq - CORES)

    @pl.when(chip < chips - 1)
    def _():
        signal(barrier, seq=my_seq + CORES)

    every[pl.ds(me * 2, 2)] = rows_ref[...].reshape(2, share // 2, width)
    ahead = (2 * chips - 2 - chip) // chips
    behind = (chip + chips - 1) // chips
    pl.semaphore_wait(barrier, 3 + ahead + behind)

    ring = ZRing(every, z_send, z_recv, n_item)
    ring.start(1)

    def project(shards):
        x = jnp.concatenate([every[pl.ds(j * 2, 2)].reshape(share, width) for j in shards], axis=0)
        normed = rms(x.astype(F32), again_ref[...]).astype(BF16)
        q = dot(normed, wq_ref[...])
        pair = dot(normed, wkv_ref[...])
        pieces = [rms(q[:, g * HD:(g + 1) * HD], qg_ref[...]).astype(BF16) for g in range(group)]
        pieces.append(rms(pair[:, :HD], kg_ref[...]).astype(BF16))
        pieces.append(pair[:, HD:].astype(BF16))
        for at, j in enumerate(shards):
            here = pl.ds(pl.multiple_of(j * share, share), share)
            for c, piece in enumerate(pieces):
                ranked[here, c * HD:(c + 1) * HD] = piece[at * share:(at + 1) * share]
            mine = every[pl.ds(j * 2, 2), :, pl.ds(pl.multiple_of(me * cols, cols), cols)]
            ranked[here, q_cols + 2 * HD:] = mine.reshape(share, cols)

    project([me])
    for hop in range(1, n_item // 2):
        ring.land(hop)
        project([ring.shard(0, hop), ring.shard(1, hop)])
    ring.land(n_item // 2)
    project([ring.shard(0, n_item // 2)])

    rank, _ = rank_of(ids_row_ref[...], ids_col_ref[...], per_dev, n_seq, 1)
    goal = (rank & (n_item - 1)) * share + rank // n_item
    order = onehot(goal == iota((rows, rows), 1))
    placed = dot(order, ranked[...]).astype(BF16)
    for g in range(group):
        query[g * rows:(g + 1) * rows] = placed[:, g * HD:(g + 1) * HD]
    kv[core] = placed[:, q_cols:q_cols + 2 * HD].reshape(2, rows // 2, 2 * HD)
    res_ref[...] = placed[:, q_cols + 2 * HD:]

    def lane_copy(hop, half):
        return remote(
            kv.at[(hop - 1) * 2 + core, half], kv.at[hop * 2 + core, half],
            lane_send.at[hop - 1, half], lane_recv.at[hop - 1, half], seq=my_seq + CORES,
        )

    def pair_copy(hop, half, lane):
        return remote(
            kv.at[hop * 2 + lane, half], kv.at[hop * 2 + lane, half],
            pair_send.at[hop, half], pair_recv.at[hop, half], seq=sibling,
        )

    not_last = chip < chips - 1

    @pl.when(not_last)
    def _():
        for half in range(2):
            lane_copy(1, half).start()

    @pl.when(core == 0)
    def _():
        for half in range(2):
            pair_copy(0, half, 0).start()

    scale = 1.4426950408889634 / HD**0.5
    tile = min(256, rows)
    tiles = group * rows // tile

    def absorb(block, key_base, first):
        def one(t, _):
            here = pl.ds(pl.multiple_of(t * tile, tile), tile)
            keys = kv[block, :, :, :HD].reshape(rows, HD)
            values = kv[block, :, :, HD:].reshape(rows, HD)
            score = lax.dot_general(
                query[here], keys, (((1,), (1,)), ((), ())), preferred_element_type=F32
            ) * scale
            key_pos = key_base + iota((1, rows), 1)
            if first:
                at = base + lax.rem(t * tile, rows) + iota((tile, 1), 0)
                allowed = (key_pos <= at) & (key_pos < length)
            else:
                allowed = key_pos < length
            score = jnp.where(allowed, score, -jnp.inf)
            old = jnp.full((tile, 1), -1e30, F32) if first else top[here]
            new = jnp.maximum(old, jnp.max(score, axis=-1, keepdims=True))
            weights = jnp.exp2(score - new)
            part = jnp.sum(weights, axis=-1, keepdims=True)
            out = dot(weights.astype(BF16), values)
            if first:
                total[here] = part
                acc[here] = out
            else:
                shrink = jnp.exp2(old - new)
                total[here] = total[here] * shrink + part
                acc[here] = acc[here] * shrink + out
            top[here] = new
            return 0

        lax.fori_loop(0, tiles, one, 0)

    absorb(core, base, True)

    @pl.when(core == 1)
    def _():
        for half in range(2):
            pair_copy(0, half, 0).wait_recv()
        absorb(0, base - rows, False)

    for hop in range(1, chips):
        @pl.when(chip >= hop)
        def _():
            for half in range(2):
                lane_copy(hop, half).wait_recv()
                if hop < chips - 1:
                    @pl.when(not_last)
                    def _():
                        lane_copy(hop + 1, half).start()
                pair_copy(hop, half, core).start()
            absorb(hop * 2 + core, base - 2 * hop * rows, False)
            for half in range(2):
                pair_copy(hop, half, other).wait_recv()
            absorb(hop * 2 + other, base - 2 * hop * rows + (other - core) * rows, False)

    for g in range(group):
        here = slice(g * rows, (g + 1) * rows)
        fine = base + iota((rows, 1), 0) < length
        attn = acc[here] / total[here]
        attn_ref[:, g * HD:(g + 1) * HD] = jnp.where(fine, attn, 0.0).astype(BF16)

    ring.drain()

    @pl.when(not_last)
    def _():
        for half in range(2):
            lane_copy(1, half).wait_send()

    @pl.when(core == 0)
    def _():
        for half in range(2):
            pair_copy(0, half, 0).wait_send()

    for hop in range(1, chips):
        @pl.when(chip >= hop)
        def _():
            for half in range(2):
                if hop < chips - 1:
                    @pl.when(not_last)
                    def _():
                        lane_copy(hop + 1, half).wait_send()
                pair_copy(hop, half, core).wait_send()


def mix_kernel(n_item, attn_ref, res_ref, wout_ref, out_ref, outgo, income, send, recv):
    me = lax.axis_index("item")
    rows = attn_ref.shape[0]
    half_rows = rows // 2
    cols = out_ref.shape[1]
    far = n_item // 2

    barrier = pltpu.get_barrier_semaphore()
    for step in (1, n_item - 1):
        signal(barrier, item=lax.rem(me + step, n_item))

    plan = []
    for way in range(2):
        steps = [(far, way)]
        for k in range(far - 1, 0, -1):
            steps += [(k, 1 - way), (k, way)]
        plan.append(steps)

    def partial(goal, half):
        here = pl.ds(pl.multiple_of(goal * cols, cols), cols)
        return dot(attn_ref[half * half_rows:(half + 1) * half_rows], wout_ref[:, here])

    def copy(way, at):
        step = 1 if way == 0 else n_item - 1
        return remote(
            outgo.at[way, at], income.at[way, at], send.at[way, at], recv.at[way, at],
            item=lax.rem(me + step, n_item),
        )

    for at in range(len(plan[0])):
        for way in range(2):
            k, half = plan[way][at]
            goal = lax.rem(me + (k if way == 0 else n_item - k), n_item)
            value = partial(goal, half)
            if (k + 1, half) in plan[way]:
                before = plan[way].index((k + 1, half))
                copy(way, before).wait_recv()
                value = value + income[way, before].astype(F32)
            outgo[way, at] = value.astype(BF16)
            if at == 0 and way == 0:
                pl.semaphore_wait(barrier, 2)
            copy(way, at).start()

    for half in (1, 0):
        here = slice(half * half_rows, (half + 1) * half_rows)
        value = partial(me, half) + res_ref[here].astype(F32)
        for way in range(2):
            if (1, half) in plan[way]:
                at = plan[way].index((1, half))
                copy(way, at).wait_recv()
                value = value + income[way, at].astype(F32)
        out_ref[here] = value.astype(BF16)
    for way in range(2):
        for at in range(len(plan[0])):
            copy(way, at).wait_send()


def vmem(count):
    return [pl.BlockSpec(memory_space=pltpu.VMEM)] * count


def params(number):
    return pltpu.CompilerParams(
        collective_id=number, has_side_effects=True, vmem_limit_bytes=VMEM_LIMIT
    )


def body(ny, item_states, item_gain, hist_ids, lengths, attn_gain, w_q, w_kv, q_gain, k_gain, w_out):
    n_seq = lax.axis_size("seq")
    n_item = lax.axis_size("item")
    nq = n_seq // ny
    per_dev, width = item_states.shape
    rows = hist_ids.shape[0]
    share = rows // n_item
    far = n_item // 2
    span = LEN // rows
    chips = span // CORES
    cols = width // n_item
    parts = 2
    dma = pltpu.SemaphoreType.DMA
    ids_row, ids_col = hist_ids.reshape(1, rows), hist_ids.reshape(rows, 1)

    fetched = pl.pallas_call(
        functools.partial(fetch_kernel, n_item, n_seq, ny),
        out_shape=jax.ShapeDtypeStruct((share, width), BF16),
        in_specs=vmem(4),
        out_specs=pl.BlockSpec(memory_space=pltpu.VMEM),
        scratch_shapes=[
            pltpu.VMEM((n_item * 2, per_dev // 2, width), BF16),
            pltpu.VMEM((ny, nq, 128), I32),
            pltpu.VMEM((ny, nq, 128), I32),
            pltpu.VMEM((nq, ny, 128), I32),
            pltpu.VMEM((nq, ny, 128), I32),
            pltpu.VMEM((parts, nq, 2 * ny, width // parts), BF16),
            pltpu.VMEM((parts, nq, 2 * ny, width // parts), BF16),
            pltpu.VMEM((parts, ny, 2 * nq, width // parts), BF16),
            pltpu.VMEM((parts, ny, 2 * nq, width // parts), BF16),
            dma((2, far, 2)), dma((2, far, 2)),
            dma((ny,)), dma((ny,)), dma((nq,)), dma((nq,)),
            dma((parts, nq)), dma((parts, nq)), dma((parts, ny)), dma((parts, ny)),
        ],
        compiler_params=params(1),
        name="fetch",
    )(ids_row, ids_col, item_states, item_gain.reshape(1, width))

    q_cols = w_q.shape[1]
    group = q_cols // HD
    attn, res = pl.pallas_call(
        functools.partial(attend_kernel, n_item, n_seq, per_dev),
        out_shape=[
            jax.ShapeDtypeStruct((rows, q_cols), BF16),
            jax.ShapeDtypeStruct((rows, cols), BF16),
        ],
        in_specs=vmem(2) + [pl.BlockSpec(memory_space=pltpu.SMEM)] + vmem(6),
        out_specs=vmem(2),
        scratch_shapes=[
            pltpu.VMEM((n_item * 2, share // 2, width), BF16),
            pltpu.VMEM((rows, q_cols + 2 * HD + cols), BF16),
            pltpu.VMEM((group * rows, HD), BF16),
            pltpu.VMEM((span, 2, rows // 2, 2 * HD), BF16),
            pltpu.VMEM((group * rows, HD), F32),
            pltpu.VMEM((group * rows, 1), F32),
            pltpu.VMEM((group * rows, 1), F32),
            dma((2, far, 2)), dma((2, far, 2)),
            dma((chips - 1, 2)), dma((chips - 1, 2)), dma((chips, 2)), dma((chips, 2)),
        ],
        compiler_params=params(2),
        name="attend",
    )(
        ids_row, ids_col, lengths, fetched, attn_gain.reshape(1, width), w_q,
        w_kv.reshape(width, 2 * HD), q_gain.reshape(1, HD), k_gain.reshape(1, HD),
    )

    steps = 2 * far - 1
    return pl.pallas_call(
        functools.partial(mix_kernel, n_item),
        out_shape=jax.ShapeDtypeStruct((rows, cols), BF16),
        in_specs=vmem(3),
        out_specs=pl.BlockSpec(memory_space=pltpu.VMEM),
        scratch_shapes=[
            pltpu.VMEM((2, steps, rows // 2, cols), BF16),
            pltpu.VMEM((2, steps, rows // 2, cols), BF16),
            dma((2, steps)), dma((2, steps)),
        ],
        compiler_params=params(3),
        name="mix",
    )(attn, res, w_out)


def solution(mesh):
    placed = (
        P(("item", "seq"), None),
        P(),
        P("seq"),
        P(),
        P(),
        P(None, "item"),
        P(None, None, "item"),
        P(),
        P(),
        P("item", None),
    )
    return jax.shard_map(
        functools.partial(body, NY),
        mesh=mesh, in_specs=placed, out_specs=P("seq", "item"), check_vma=False,
    )
```

time: 269 us -> 130 us (0.48)
  waiting for transfers between devices: 126 us -> 0 us
  Pallas kernels: 0 us -> 125 us
  starting transfers between devices: 46.5 us -> 0 us
  blocking collectives: 22.6 us -> 0 us
  local copies, waits for them, and re-layouts: 22.9 us -> 4.42 us
  other arithmetic: 17.8 us -> 0 us
  matrix products: 17.1 us -> 0 us
  between operations: 13.8 us -> 0.09 us
    pallas_call x0 -> x3, Pallas kernels: none -> 125 us  [the longest x1 52.1 us: body(): pl.pallas_call(functools.partial(attend_kernel, n_item, n_seq, per_dev),...]
    all_gather x1 -> x0, waiting for transfers between devices: 56.2 us -> none  [body(): lax.all_gather(fetched, 'item', axis=0, tiled=True).reshape(-1, width)]
    reduce_scatter x1 -> x0, waiting for transfers between devices: 48.7 us -> none  [body(): lax.psum_scatter(proj.astype(jnp.bfloat16), 'item', scatter_dimension=1,...]
    ppermute x7 -> x0, starting transfers between devices: 36.4 us -> none  [from_behind(): lax.ppermute(value, axis, [(source, source + steps) for source in range(f...]
    all_to_all x1 -> x0, blocking collectives: 22.6 us -> none  [body(): lax.all_to_all(found, 'seq', split_axis=0, concat_axis=0, tiled=True)]
    dot_general x19 -> x0, matrix products: 16.3 us -> none  [the longest x8 7.53 us: absorb(): jnp.einsum('kgrs,skc->kgrc', weights.astype(jnp.bfloat16), pair[1], prefe...]
    ppermute x7 -> x0, waiting for transfers between devices: 15.3 us -> none  [from_behind(): lax.ppermute(value, axis, [(source, source + steps) for source in range(f...]
    all_to_all x1 -> x0, starting transfers between devices: 9.89 us -> none  [body(): lax.all_to_all(wanted, 'seq', split_axis=0, concat_axis=0, tiled=True)]
  transfers between devices with their start and end apart: 10 -> 0, of which waited for: 10 -> 0; matrix products, arithmetic and copies ran while one was open for 4% -> 0% of each run, Pallas kernels for 0% -> 0%
where the time goes in v1:
time: 130 us
  Pallas kernels  125 us (96%)
  local copies, waits for them, and re-layouts  4.42 us (3%)
    pallas_call x1, Pallas kernels, body(): pl.pallas_call(functools.partial(attend_kernel, n_item, n_seq, per_dev),...  52.1 us
    pallas_call x1, Pallas kernels, body(): pl.pallas_call(functools.partial(fetch_kernel, n_item, n_seq, ny), out_sh...  48.6 us
    pallas_call x1, Pallas kernels, body(): pl.pallas_call(functools.partial(mix_kernel, n_item), out_shape=jax.Shape...  24.3 us
    unnamed x20, local copies, waits for them, and re-layouts  4.28 us

profile of v1, /device:TPU:56, one launch (start us, length us, event | category | flops | bytes accessed | tf_op | source)
XLA Modules:
  0.0 129.5 jit_solution(6697845132402659571)
XLA Ops:
  0.0 0.0 copy-start.3
  0.0 0.7 copy-done.3
  0.7 0.0 copy-start.2
  0.7 0.0 copy-start.5
  0.7 0.1 copy.12.ids_col_ref
  0.8 0.7 copy-done.2
  1.6 0.0 copy-done.5
  1.6 48.6 %fetch.1.rows_ref = bf16[64,2048]{1,0:T(8,128)(2,1)S(1)} custom-call(s32[1,512]{1,0:T(1,128)S(1)} %bitcast.12, s32[512,1]{1,0:T(8,128)S(1)} %copy.12.ids_col_ref, bf16[32,2048]{1,0:T(8,128)(2,1)S(1)} %copy-done.2, f32[1,2048]{1,0:T(1,128)S(1)} %bitcast.15), custom_call_target="tpu_custom_call" | custom-call | tf_op jit(solution)/shard_map/fetch/pallas_call | solution.py:526
  50.2 0.0 copy-start.1
  50.3 0.0 copy-start.4
  50.3 1.4 %copy.15 = bf16[256,8,2,128]{3,1,2,0:T(8,128)(2,1)S(1)} copy(bf16[256,8,2,128]{3,2,1,0:T(2,128)(2,1)} %bitcast.18) | data formatting | bytes 2097152
  51.7 0.0 copy-start.6
  51.7 0.0 copy-start.7
  51.7 0.0 copy-start.8
  51.8 0.0 copy-done.1
  51.8 0.0 copy-done.4
  51.8 0.6 copy-done.6
  52.4 0.0 copy-done.7
  52.4 0.0 copy-done.8
  52.4 0.0 copy-start
  52.4 52.1 %attend.1 = (bf16[512,256]{1,0:T(8,128)(2,1)S(1)}, bf16[512,256]{1,0:T(8,128)(2,1)S(1)}) custom-call(s32[1,512]{1,0:T(1,128)S(1)} %bitcast.13, s32[512,1]{1,0:T(8,128)S(1)} %copy.12.ids_col_ref, s32[8]{0:T(128)S(1)} %copy-done.6, bf16[64,2048]{1,0:T(8,128)(2,1)S(1)} %fetch.1.rows_ref, f32[1,2048]{1,0:T(1,128)S(1)} %bitcast.14, ...), custom_call_target="tpu_custom_call" | custom-call | tf_op jit(solution)/shard_map/attend/pallas_call | solution.py:551
  104.5 0.0 copy-done
  104.5 24.3 %mix.1 = bf16[512,256]{1,0:T(8,128)(2,1)S(1)} custom-call(bf16[512,256]{1,0:T(8,128)(2,1)S(1)} %get-tuple-element.7.attn_ref, bf16[512,256]{1,0:T(8,128)(2,1)S(1)} %get-tuple-element.8.res_ref, bf16[256,2048]{1,0:T(8,128)(2,1)S(1)} %copy-done), custom_call_target="tpu_custom_call" | custom-call | tf_op jit(solution)/shard_map/mix/pallas_call | solution.py:578
  128.8 0.7 copy.17
Async XLA Ops:
  0.0 0.7 copy-start.3
  0.7 0.9 copy-start.2
  0.7 0.9 copy-start.5
  50.2 1.5 %copy-start.1 = (bf16[2048,256]{1,0:T(8,128)(2,1)S(1)}, bf16[2048,256]{1,0:T(8,128)(2,1)}, u32[]{:S(2)}) copy-start(bf16[2048,256]{1,0:T(8,128)(2,1)} %wq_ref.1) | copy-start | bytes 3145732
  50.3 1.5 %copy-start.4 = (f32[2048]{0:T(1024)S(1)}, f32[2048]{0:T(1024)}, u32[]{:S(2)}) copy-start(f32[2048]{0:T(1024)} %param.14) | copy-start | bytes 24580
  51.7 0.7 copy-start.6
  51.7 0.7 copy-start.7
  51.7 0.7 copy-start.8
  52.4 52.1 %copy-start = (bf16[256,2048]{1,0:T(8,128)(2,1)S(1)}, bf16[256,2048]{1,0:T(8,128)(2,1)}, u32[]{:S(2)}) copy-start(bf16[256,2048]{1,0:T(8,128)(2,1)} %wout_ref.1) | copy-start | bytes 3145732

commit v2 on v0

v2 whole, which is shorter than its diff:
```python
import functools

import jax
import jax.numpy as jnp
from jax import lax
from jax.experimental import pallas as pl
from jax.experimental.pallas import tpu as pltpu
from jax.sharding import PartitionSpec as P

HD = 128
LEN = 4096
CORES = 2
PARTS = 4
NY = 8
F32, BF16, I32 = jnp.float32, jnp.bfloat16, jnp.int32
VMEM_LIMIT = 48 * 1024 * 1024


def rms(x, gain):
    return x * lax.rsqrt(jnp.mean(x * x, axis=-1, keepdims=True) + 1e-06) * gain


def iota(shape, dim):
    return lax.broadcasted_iota(I32, shape, dim)


def onehot(mask):
    return jnp.where(mask, 1.0, 0.0).astype(BF16)


def dot(a, b):
    return jnp.dot(a, b, preferred_element_type=F32)


def signal(sem, **where):
    pl.semaphore_signal(sem, inc=1, device_id=where, device_id_type=pl.DeviceIdType.MESH)


def remote(src, dst, send, recv, **where):
    return pltpu.make_async_remote_copy(
        src_ref=src, dst_ref=dst, send_sem=send, recv_sem=recv,
        device_id=where, device_id_type=pl.DeviceIdType.MESH,
    )


class ZRing:
    def __init__(self, piece, send, recv, n):
        self.piece, self.send, self.recv, self.n = piece, send, recv, n
        self.far = n // 2
        self.me = lax.axis_index("item")

    def copy(self, way, part, hop, shard):
        step = 1 if way == 0 else self.n - 1
        ref = self.piece(part, shard, way if hop == self.far else None)
        at = (way, part, hop - 1)
        return remote(
            ref, ref, self.send.at[at], self.recv.at[at], item=lax.rem(self.me + step, self.n)
        )

    def shard(self, way, hop):
        return lax.rem(self.me + (self.n - hop if way == 0 else hop), self.n)

    def start(self, part):
        for way in range(2):
            self.copy(way, part, 1, self.me).start()

    def land(self, part, hop):
        for way in range(2):
            self.copy(way, part, hop, self.shard(way, hop)).wait_recv()
            if hop < self.far:
                self.copy(way, part, hop + 1, self.shard(way, hop)).start()

    def drain(self, parts):
        for part in range(parts):
            for hop in range(1, self.far + 1):
                for way in range(2):
                    self.copy(way, part, hop, self.shard(way, hop - 1)).wait_send()


def rank_of(ids_row, ids_col, per_dev, n_seq, axis):
    rows = ids_row.shape[1]
    owner_row = (ids_row // per_dev) & (n_seq - 1)
    owner_col = (ids_col // per_dev) & (n_seq - 1)
    lane, sub = iota((rows, rows), 1), iota((rows, rows), 0)
    if axis == 0:
        same = (owner_col == owner_row) & (sub < lane)
        less = owner_col < owner_row
    else:
        same = (owner_col == owner_row) & (lane < sub)
        less = owner_row < owner_col
    within = jnp.sum(jnp.where(same, 1.0, 0.0), axis=axis, keepdims=True).astype(I32)
    before = jnp.sum(jnp.where(less, 1.0, 0.0), axis=axis, keepdims=True).astype(I32)
    return before + within, within


def kernel(
    n_item, n_seq, ny, ids_row_ref, ids_col_ref, len_ref, states_ref, igain_ref, again_ref,
    qg_ref, kg_ref, wq_hbm, wkv_hbm, wout_hbm, out_ref,
    wq_ref, wkv_ref, wout_ref, table, id_a, id_b, id_c, id_d, found, mid, turned, final,
    every, sums, squares, mine, order, query, kv, bias, acc, top, total, attn_ref, res_ref, outgo, income,
    w_sem, t_send, t_recv, iy_send, iy_recv, ix_send, ix_recv, rx_send, rx_recv, ry_send, ry_recv,
    z_send, z_recv, lane_send, lane_recv, pair_send, pair_recv, o_send, o_recv,
):
    nq = n_seq // ny
    far = n_item // 2
    me = lax.axis_index("item")
    my_seq = lax.axis_index("seq")
    core = lax.rem(my_seq, CORES)
    other = 1 - core
    sibling = my_seq + 1 - 2 * core
    my_y = lax.rem(my_seq // CORES, ny)
    my_x = my_seq // (CORES * ny)
    my_q = my_x * CORES + core
    per_dev, width = states_ref.shape
    rows = ids_row_ref.shape[1]
    share = rows // n_item
    span = LEN // rows
    chips = span // CORES
    chip = lax.rem(my_seq // CORES, chips)
    not_last = chip < chips - 1
    base = lax.rem(my_seq, span) * rows
    length = len_ref[my_seq // span]
    q_cols = wq_ref.shape[1]
    group = q_cols // HD
    out_cols = width // n_item
    parts = found.shape[0]
    cols = width // parts

    def along_y(y):
        return (my_x * ny + y) * CORES + core

    def along_q(q):
        return ((q // CORES) * ny + my_y) * CORES + lax.rem(q, CORES)

    def y_plus(d):
        return lax.rem(my_y + d, ny)

    def q_plus(d):
        return lax.rem(my_q + d, nq)

    barrier = pltpu.get_barrier_semaphore()
    for step in (1, n_item - 1):
        signal(barrier, item=lax.rem(me + step, n_item))
    for d in range(1, ny):
        signal(barrier, seq=along_y(y_plus(d)))
    for d in range(1, nq):
        signal(barrier, seq=along_q(q_plus(d)))

    weights = [
        pltpu.make_async_copy(wq_hbm, wq_ref, w_sem.at[0]),
        pltpu.make_async_copy(wkv_hbm, wkv_ref, w_sem.at[1]),
        pltpu.make_async_copy(wout_hbm, wout_ref, w_sem.at[2]),
    ]
    for copy in weights:
        copy.start()

    embed = rms(states_ref[...].astype(F32), igain_ref[...]).astype(BF16)
    table[pl.ds(me * 2, 2)] = embed.reshape(2, per_dev // 2, width)
    pl.semaphore_wait(barrier, 2 + (ny - 1) + (nq - 1))

    def table_piece(part, shard, half):
        return table.at[pl.ds(shard * 2, 2)] if half is None else table.at[shard * 2 + half]

    items_ring = ZRing(table_piece, t_send, t_recv, n_item)
    items_ring.start(0)

    ids_row, ids_col = ids_row_ref[...], ids_col_ref[...]
    rank, within = rank_of(ids_row, ids_col, per_dev, n_seq, 0)
    owner = ids_row // per_dev
    owner_seq = owner & (n_seq - 1)
    source_y = (owner_seq // CORES) & (ny - 1)
    source_q = (owner_seq // (CORES * ny)) * CORES + (owner_seq & (CORES - 1))
    item = (owner // n_seq) * per_dev + (ids_row & (per_dev - 1)) + 1
    asks = (rank & (n_item - 1)) == me
    copy_no = within // n_item
    place = jnp.where(asks, source_y * nq + source_q, -1)
    asked = []
    for sub in range(2):
        hit = (iota((ny * nq, rows), 0) == place) & (copy_no == sub)
        asked.append(jnp.sum(jnp.where(hit, item.astype(F32), 0.0), axis=1, keepdims=True).astype(I32))
    lanes = iota((ny * nq, 128), 1)
    id_a[...] = jnp.where(lanes == 0, asked[0], jnp.where(lanes == 1, asked[1], 0)).reshape(ny, nq, 128)

    def ids_y(d, y_from, y_to):
        return remote(
            id_a.at[y_to], id_b.at[y_from], iy_send.at[d - 1], iy_recv.at[d - 1], seq=along_y(y_to)
        )

    def ids_q(d, q_from, q_to):
        return remote(
            id_c.at[q_to], id_d.at[q_from], ix_send.at[d - 1], ix_recv.at[d - 1], seq=along_q(q_to)
        )

    for d in range(1, ny):
        ids_y(d, my_y, y_plus(d)).start()
    id_b[my_y] = id_a[my_y]

    spot = jnp.where(asks, rank // n_item, -1)
    pick_a = onehot(iota((share, rows), 0) == spot)
    pick_b = onehot(iota((ny * nq * 2, rows), 0) == jnp.where(asks, place * 2 + copy_no, -1))
    pick = lax.dot_general(pick_a, pick_b, (((1,), (1,)), ((), ())), preferred_element_type=F32).astype(BF16)
    to, frm = iota((ny * nq * 2, nq * 2 * ny), 0), iota((ny * nq * 2, nq * 2 * ny), 1)
    to_y, to_q, to_sub = to // (nq * 2), (to // 2) % nq, to % 2
    turn = onehot(frm == (to_q * 2 + to_sub) * ny + to_y)

    for d in range(1, ny):
        ids_y(d, y_plus(ny - d), my_y).wait_recv()
    for q in range(nq):
        id_c[q] = id_b[:, q, :]
    for d in range(1, nq):
        ids_q(d, my_q, q_plus(d)).start()
    id_d[my_q] = id_c[my_q]
    items_ring.land(0, 1)

    def landing(rank):
        apart = (rank - me + n_item) & (n_item - 1)
        place = jnp.where(apart == 0, 0, jnp.where(apart < far, 2 * apart, 2 * (n_item - apart) - 1))
        return place * share + rank // n_item

    goal_row = landing(rank)
    pos_col = jnp.sum(
        jnp.where(goal_row == iota((rows, rows), 0), iota((rows, rows), 1).astype(F32), 0.0), axis=1, keepdims=True
    ).astype(I32)
    rank_col, _ = rank_of(ids_row, ids_col, per_dev, n_seq, 1)
    placed = landing(rank_col) == iota((rows, rows), 1)
    order[...] = onehot(placed)
    pos_row = jnp.sum(jnp.where(placed, iota((rows, rows), 0).astype(F32), 0.0), axis=0, keepdims=True).astype(I32)
    bias[core] = jnp.broadcast_to(jnp.where(base + pos_row < length, 0.0, -jnp.inf), (8, rows))
    items_ring.land(0, 2) if far > 1 else None

    chunks = [slice(0, 3 * share if far > 1 else 2 * share)]
    for hop in range(2, far + 1):
        chunks.append(slice((2 * hop - 1) * share, min(2 * hop + 1, n_item) * share))
    n_chunks = len(chunks)

    def block(slot, c):
        if c < 0:
            return bias.at[slot]
        return kv.at[slot, pl.ds(chunks[c].start, chunks[c].stop - chunks[c].start)]

    def lane_copy(hop, c):
        return remote(
            block((hop - 1) * 2 + core, c), block(hop * 2 + core, c),
            lane_send.at[hop - 1, c + 1], lane_recv.at[hop - 1, c + 1], seq=my_seq + CORES,
        )

    def pair_copy(hop, c, lane):
        return remote(
            block(hop * 2 + lane, c), block(hop * 2 + lane, c),
            pair_send.at[hop, c + 1], pair_recv.at[hop, c + 1], seq=sibling,
        )

    def give(c):
        @pl.when(not_last)
        def _():
            lane_copy(1, c).start()

        @pl.when(core == 0)
        def _():
            pair_copy(0, c, 0).start()

    def pass_on(stage):
        for hop in range(1, chips):
            c = stage - hop
            if -1 <= c < n_chunks:
                @pl.when(chip >= hop)
                def _():
                    lane_copy(hop, c).wait_recv()
                    if hop < chips - 1:
                        @pl.when(not_last)
                        def _():
                            lane_copy(hop + 1, c).start()
                    pair_copy(hop, c, core).start()

    give(-1)
    for hop in range(3, far + 1):
        items_ring.land(0, hop)

    for d in range(1, nq):
        ids_q(d, q_plus(nq - d), my_q).wait_recv()
    wanted = id_d[...].reshape(nq * ny, 128)
    names = iota((nq * ny, n_item * per_dev), 1) + 1
    choose = jnp.stack(
        [jnp.where(wanted[:, sub:sub + 1] == names, 1.0, 0.0).reshape(nq, ny, n_item * per_dev) for sub in range(2)],
        axis=1,
    ).reshape(nq * 2 * ny, n_item * per_dev).astype(BF16)

    def rows_q(part, d, q_from, q_to):
        return remote(
            found.at[part, q_to], mid.at[part, q_from],
            rx_send.at[part, d - 1], rx_recv.at[part, d - 1], seq=along_q(q_to),
        )

    def rows_y(part, d, y_from, y_to):
        return remote(
            turned.at[part, y_to], final.at[part, y_from],
            ry_send.at[part, d - 1], ry_recv.at[part, d - 1], seq=along_y(y_to),
        )

    for part in range(parts):
        source = table[:, :, part * cols:(part + 1) * cols].reshape(n_item * per_dev, cols)
        found[part] = dot(choose, source).astype(BF16).reshape(nq, 2 * ny, cols)
        for d in range(1, nq):
            rows_q(part, d, my_q, q_plus(d)).start()
        mid[part, my_q] = found[part, my_q]
    for part in range(parts):
        for d in range(1, nq):
            rows_q(part, d, q_plus(nq - d), my_q).wait_recv()
        turned[part] = dot(turn, mid[part].reshape(nq * 2 * ny, cols)).astype(BF16).reshape(ny, 2 * nq, cols)
        for d in range(1, ny):
            rows_y(part, d, my_y, y_plus(d)).start()
        final[part, my_y] = turned[part, my_y]

    def rows_piece(part, shard, half):
        return every.at[part, pl.ds(shard * 2, 2)] if half is None else every.at[part, shard * 2 + half]

    ring = ZRing(rows_piece, z_send, z_recv, n_item)

    def arrive(part):
        for d in range(1, ny):
            rows_y(part, d, y_plus(ny - d), my_y).wait_recv()
        got = dot(pick, final[part].reshape(ny * 2 * nq, cols)).astype(BF16)
        every[part, pl.ds(me * 2, 2)] = got.reshape(2, share // 2, cols)
        ring.start(part)

    def project(part, hop):
        shards = [me] if hop == 0 else [ring.shard(0, hop)] + ([ring.shard(1, hop)] if hop < far else [])
        first = 0 if hop == 0 else (2 * hop - 1) * share
        here = slice(first, first + len(shards) * share)
        x = jnp.concatenate([every[part, pl.ds(j * 2, 2)].reshape(share, cols) for j in shards], axis=0).astype(F32)
        span = slice(part * cols, (part + 1) * cols)
        y = (x * again_ref[:, span]).astype(BF16)
        q = dot(y, wq_ref[span])
        pair = dot(y, wkv_ref[span])
        square = jnp.sum(x * x, axis=-1, keepdims=True)
        if part > 0:
            q = q + sums[here, :q_cols]
            pair = pair + sums[here, q_cols:]
            square = square + squares[here]
        if part < parts - 1:
            sums[here, :q_cols] = q
            sums[here, q_cols:] = pair
            squares[here] = square
            return
        scale = lax.rsqrt(square / width + 1e-06)
        q, pair = q * scale, pair * scale
        for g in range(group):
            query[g * rows + here.start:g * rows + here.stop] = rms(q[:, g * HD:(g + 1) * HD], qg_ref[...]).astype(BF16)
        kv[core, here, :HD] = rms(pair[:, :HD], kg_ref[...]).astype(BF16)
        kv[core, here, HD:] = pair[:, HD:].astype(BF16)

    def projected(part, hop):
        project(part, hop)
        if part == parts - 1 and hop > 0:
            give(hop - 1)
            pass_on(hop - 1)

    for diagonal in range(parts + far):
        now = [(part, diagonal - part) for part in range(parts) if 1 <= diagonal - part <= far]
        for part, hop in now:
            ring.land(part, hop)
        if diagonal < parts:
            arrive(diagonal)
        if diagonal == 0:
            for copy in weights:
                copy.wait()
        for part, hop in now:
            projected(part, hop)
        if diagonal < parts:
            projected(diagonal, 0)

    scale = 1.4426950408889634 / HD**0.5

    def absorb(blocks, first):
        for g in range(group):
            here = slice(g * rows, (g + 1) * rows)
            q = query[here]
            if first:
                old = jnp.full((rows, 1), -1e30, F32)
            else:
                old, whole, out = top[here], total[here], acc[here]
            for slot in blocks:
                score = lax.dot_general(
                    q, kv[slot, :, :HD], (((1,), (1,)), ((), ())), preferred_element_type=F32
                ) * scale + bias[slot, 0:1]
                if first:
                    score = jnp.where(pos_row <= pos_col, score, -jnp.inf)
                new = jnp.maximum(old, jnp.max(score, axis=-1, keepdims=True))
                weights = jnp.exp2(score - new)
                part = jnp.sum(weights, axis=-1, keepdims=True)
                more = dot(weights.astype(BF16), kv[slot, :, HD:])
                if first:
                    whole, out = part, more
                else:
                    shrink = jnp.exp2(old - new)
                    whole, out = whole * shrink + part, out * shrink + more
                old = new
            top[here], total[here], acc[here] = old, whole, out

    stage = far
    absorb([core], True)
    pass_on(stage)

    @pl.when(core == 1)
    def _():
        for c in range(-1, n_chunks):
            pair_copy(0, c, 0).wait_recv()
        absorb([0], False)

    for hop in range(1, chips):
        stage += 1
        pass_on(stage)

        @pl.when(chip >= hop)
        def _():
            for c in range(-1, n_chunks):
                pair_copy(hop, c, other).wait_recv()
            absorb([hop * 2 + core, hop * 2 + other], False)

    seen = jnp.concatenate(
        [(acc[g * rows:(g + 1) * rows] / total[g * rows:(g + 1) * rows]).astype(BF16) for g in range(group)], axis=1
    )
    fine = base + iota((rows, 1), 0) < length
    attn_ref[...] = jnp.where(fine, dot(order[...], seen), 0.0).astype(BF16)

    half_rows = rows // 2
    plan = []
    for way in range(2):
        steps = [(far, way)]
        for k in range(far - 1, 0, -1):
            steps += [(k, 1 - way), (k, way)]
        plan.append(steps)

    def partial(goal, half):
        here = pl.ds(pl.multiple_of(goal * out_cols, out_cols), out_cols)
        return dot(attn_ref[half * half_rows:(half + 1) * half_rows], wout_ref[:, here])

    def sum_copy(way, at):
        step = 1 if way == 0 else n_item - 1
        return remote(
            outgo.at[way, at], income.at[way, at], o_send.at[way, at], o_recv.at[way, at],
            item=lax.rem(me + step, n_item),
        )

    for at in range(len(plan[0])):
        for way in range(2):
            k, half = plan[way][at]
            goal = lax.rem(me + (k if way == 0 else n_item - k), n_item)
            value = partial(goal, half)
            if (k + 1, half) in plan[way]:
                before = plan[way].index((k + 1, half))
                sum_copy(way, before).wait_recv()
                value = value + income[way, before].astype(F32)
            outgo[way, at] = value.astype(BF16)
            sum_copy(way, at).start()
        if at == min(1, len(plan[0]) - 1):
            where = me * out_cols
            inside = pl.ds(pl.multiple_of(lax.rem(where, cols), out_cols), out_cols)
            for hop in range(far + 1):
                for way in range(2 if 0 < hop < far else 1):
                    j = ring.shard(way, hop) if hop > 0 else me
                    first = 0 if hop == 0 else (2 * hop - 1 + way) * share
                    mine[first:first + share] = every[where // cols, pl.ds(j * 2, 2), :, inside].reshape(share, out_cols)
            res_ref[...] = dot(order[...], mine[...]).astype(BF16)

    for half in (1, 0):
        here = slice(half * half_rows, (half + 1) * half_rows)
        value = partial(me, half) + res_ref[here].astype(F32)
        for way in range(2):
            if (1, half) in plan[way]:
                at = plan[way].index((1, half))
                sum_copy(way, at).wait_recv()
                value = value + income[way, at].astype(F32)
        out_ref[here] = value.astype(BF16)

    items_ring.drain(1)
    ring.drain(parts)
    for d in range(1, ny):
        ids_y(d, my_y, y_plus(d)).wait_send()
    for d in range(1, nq):
        ids_q(d, my_q, q_plus(d)).wait_send()
    for part in range(parts):
        for d in range(1, nq):
            rows_q(part, d, my_q, q_plus(d)).wait_send()
        for d in range(1, ny):
            rows_y(part, d, my_y, y_plus(d)).wait_send()
    for c in range(-1, n_chunks):
        @pl.when(not_last)
        def _():
            lane_copy(1, c).wait_send()

        @pl.when(core == 0)
        def _():
            pair_copy(0, c, 0).wait_send()

        for hop in range(1, chips):
            @pl.when(chip >= hop)
            def _():
                if hop < chips - 1:
                    @pl.when(not_last)
                    def _():
                        lane_copy(hop + 1, c).wait_send()
                pair_copy(hop, c, core).wait_send()
    for way in range(2):
        for at in range(len(plan[0])):
            sum_copy(way, at).wait_send()


def body(ny, item_states, item_gain, hist_ids, lengths, attn_gain, w_q, w_kv, q_gain, k_gain, w_out):
    n_seq = lax.axis_size("seq")
    n_item = lax.axis_size("item")
    nq = n_seq // ny
    per_dev, width = item_states.shape
    rows = hist_ids.shape[0]
    share = rows // n_item
    far = n_item // 2
    span = LEN // rows
    chips = span // CORES
    out_cols = width // n_item
    q_cols = w_q.shape[1]
    group = q_cols // HD
    cols = width // PARTS
    steps = 2 * far - 1
    dma = pltpu.SemaphoreType.DMA
    vmem, smem, hbm = (pl.BlockSpec(memory_space=space) for space in (pltpu.VMEM, pltpu.SMEM, pl.ANY))
    return pl.pallas_call(
        functools.partial(kernel, n_item, n_seq, ny),
        out_shape=jax.ShapeDtypeStruct((rows, out_cols), BF16),
        in_specs=[vmem] * 2 + [smem] + [vmem] * 5 + [hbm] * 3,
        out_specs=vmem,
        scratch_shapes=[
            pltpu.VMEM((width, q_cols), BF16),
            pltpu.VMEM((width, 2 * HD), BF16),
            pltpu.VMEM((q_cols, width), BF16),
            pltpu.VMEM((n_item * 2, per_dev // 2, width), BF16),
            pltpu.VMEM((ny, nq, 128), I32),
            pltpu.VMEM((ny, nq, 128), I32),
            pltpu.VMEM((nq, ny, 128), I32),
            pltpu.VMEM((nq, ny, 128), I32),
            pltpu.VMEM((PARTS, nq, 2 * ny, cols), BF16),
            pltpu.VMEM((PARTS, nq, 2 * ny, cols), BF16),
            pltpu.VMEM((PARTS, ny, 2 * nq, cols), BF16),
            pltpu.VMEM((PARTS, ny, 2 * nq, cols), BF16),
            pltpu.VMEM((PARTS, n_item * 2, share // 2, cols), BF16),
            pltpu.VMEM((rows, q_cols + 2 * HD), F32),
            pltpu.VMEM((rows, 1), F32),
            pltpu.VMEM((rows, out_cols), BF16),
            pltpu.VMEM((rows, rows), BF16),
            pltpu.VMEM((group * rows, HD), BF16),
            pltpu.VMEM((span, rows, 2 * HD), BF16),
            pltpu.VMEM((span, 8, rows), F32),
            pltpu.VMEM((group * rows, HD), F32),
            pltpu.VMEM((group * rows, 1), F32),
            pltpu.VMEM((group * rows, 1), F32),
            pltpu.VMEM((rows, q_cols), BF16),
            pltpu.VMEM((rows, out_cols), BF16),
            pltpu.VMEM((2, steps, rows // 2, out_cols), BF16),
            pltpu.VMEM((2, steps, rows // 2, out_cols), BF16),
            dma((3,)),
            dma((2, 1, far)), dma((2, 1, far)),
            dma((ny,)), dma((ny,)), dma((nq,)), dma((nq,)),
            dma((PARTS, nq)), dma((PARTS, nq)), dma((PARTS, ny)), dma((PARTS, ny)),
            dma((2, PARTS, far)), dma((2, PARTS, far)),
            dma((chips - 1, far + 1)), dma((chips - 1, far + 1)),
            dma((chips, far + 1)), dma((chips, far + 1)),
            dma((2, steps)), dma((2, steps)),
        ],
        compiler_params=pltpu.CompilerParams(
            collective_id=1, has_side_effects=True, vmem_limit_bytes=VMEM_LIMIT
        ),
        name="user_layer",
    )(
        hist_ids.reshape(1, rows), hist_ids.reshape(rows, 1), lengths, item_states,
        item_gain.reshape(1, width), attn_gain.reshape(1, width), q_gain.reshape(1, HD),
        k_gain.reshape(1, HD), w_q, w_kv.reshape(width, 2 * HD), w_out,
    )


def solution(mesh):
    placed = (
        P(("item", "seq"), None),
        P(),
        P("seq"),
        P(),
        P(),
        P(None, "item"),
        P(None, None, "item"),
        P(),
        P(),
        P("item", None),
    )
    return jax.shard_map(
        functools.partial(body, NY),
        mesh=mesh, in_specs=placed, out_specs=P("seq", "item"), check_vma=False,
    )
```

time: 269 us -> 126 us (0.47)
  waiting for transfers between devices: 126 us -> 0 us
  Pallas kernels: 0 us -> 121 us
  starting transfers between devices: 46.5 us -> 0 us
  blocking collectives: 22.6 us -> 0 us
  local copies, waits for them, and re-layouts: 22.9 us -> 3.76 us
  other arithmetic: 17.8 us -> 0 us
  matrix products: 17.1 us -> 0 us
  between operations: 13.8 us -> 0.1 us
    pallas_call x0 -> x1, Pallas kernels: none -> 121 us  [body(): pl.pallas_call(functools.partial(kernel, n_item, n_seq, ny), out_shape=ja...]
    all_gather x1 -> x0, waiting for transfers between devices: 56.2 us -> none  [body(): lax.all_gather(fetched, 'item', axis=0, tiled=True).reshape(-1, width)]
    reduce_scatter x1 -> x0, waiting for transfers between devices: 48.7 us -> none  [body(): lax.psum_scatter(proj.astype(jnp.bfloat16), 'item', scatter_dimension=1,...]
    ppermute x7 -> x0, starting transfers between devices: 36.4 us -> none  [from_behind(): lax.ppermute(value, axis, [(source, source + steps) for source in range(f...]
    all_to_all x1 -> x0, blocking collectives: 22.6 us -> none  [body(): lax.all_to_all(found, 'seq', split_axis=0, concat_axis=0, tiled=True)]
    dot_general x19 -> x0, matrix products: 16.3 us -> none  [the longest x8 7.53 us: absorb(): jnp.einsum('kgrs,skc->kgrc', weights.astype(jnp.bfloat16), pair[1], prefe...]
    ppermute x7 -> x0, waiting for transfers between devices: 15.3 us -> none  [from_behind(): lax.ppermute(value, axis, [(source, source + steps) for source in range(f...]
    all_to_all x1 -> x0, starting transfers between devices: 9.89 us -> none  [body(): lax.all_to_all(wanted, 'seq', split_axis=0, concat_axis=0, tiled=True)]
  transfers between devices with their start and end apart: 10 -> 0, of which waited for: 10 -> 0; matrix products, arithmetic and copies ran while one was open for 4% -> 0% of each run, Pallas kernels for 0% -> 0%
where the time goes in v2:
time: 126 us; the launch traced here: 124 us
  Pallas kernels  121 us (96%)
  local copies, waits for them, and re-layouts  3.76 us (3%)
    pallas_call x1, Pallas kernels, body(): pl.pallas_call(functools.partial(kernel, n_item, n_seq, ny), out_shape=ja...  121 us
    unnamed x20, local copies, waits for them, and re-layouts  3.62 us

profile of v2, /device:TPU:56, one launch (start us, length us, event | category | flops | bytes accessed | tf_op | source)
XLA Modules:
  0.0 124.4 jit_solution(6932405696828398244)
XLA Ops:
  0.0 0.0 copy-start.5
  0.0 0.7 copy-done.5
  0.7 0.0 copy-start.2
  0.7 0.0 copy-start.3
  0.7 0.0 copy-start.4
  0.7 0.1 copy.11.ids_col_ref
  0.8 0.0 copy-start
  0.9 0.0 copy-start.1
  0.9 1.5 %copy.14 = bf16[256,8,2,128]{3,1,2,0:T(8,128)(2,1)S(1)} copy(bf16[256,8,2,128]{3,2,1,0:T(2,128)(2,1)} %bitcast.17) | data formatting | bytes 2097152
  2.4 0.0 copy-start.6
  2.4 0.0 copy-start.7
  2.4 0.0 copy-start.8
  2.4 0.0 copy-done.2
  2.4 0.0 copy-done.3
  2.4 0.0 copy-done.4
  2.4 0.0 copy-done
  2.5 0.3 copy-done.1
  2.7 0.4 copy-done.6
  3.1 0.0 copy-done.7
  3.1 0.0 copy-done.8
  3.1 120.6 %user_layer.1 = bf16[512,256]{1,0:T(8,128)(2,1)S(1)} custom-call(s32[1,512]{1,0:T(1,128)S(1)} %bitcast.14, s32[512,1]{1,0:T(8,128)S(1)} %copy.11.ids_col_ref, s32[8]{0:T(128)S(1)} %copy-done.6, bf16[32,2048]{1,0:T(8,128)(2,1)S(1)} %copy-done.2, f32[1,2048]{1,0:T(1,128)S(1)} %bitcast.11, f32[1,2048]{1,0:T(1,128)S(1)} %bitcast.12, f32[1,128]{1,0:T(1,128)S(1)} %bitcast.15, ...), custom_call_target="tpu_custom_call" | custom-call | tf_op jit(solution)/shard_map/user_layer/pallas_call | solution.py:526
  123.7 0.7 copy.16
Async XLA Ops:
  0.0 0.7 copy-start.5
  0.7 1.7 %copy-start.2 = (bf16[32,2048]{1,0:T(8,128)(2,1)S(1)}, bf16[32,2048]{1,0:T(8,128)(2,1)}, u32[]{:S(2)}) copy-start(bf16[32,2048]{1,0:T(8,128)(2,1)} %states_ref.1) | copy-start | bytes 393220
  0.7 1.7 %copy-start.3 = (f32[2048]{0:T(1024)S(1)}, f32[2048]{0:T(1024)}, u32[]{:S(2)}) copy-start(f32[2048]{0:T(1024)} %param.11) | copy-start | bytes 24580
  0.7 1.7 %copy-start.4 = (f32[2048]{0:T(1024)S(1)}, f32[2048]{0:T(1024)}, u32[]{:S(2)}) copy-start(f32[2048]{0:T(1024)} %param.14) | copy-start | bytes 24580
  0.8 1.6 %copy-start = (bf16[2048,256]{1,0:T(8,128)(2,1)S(1)}, bf16[2048,256]{1,0:T(8,128)(2,1)}, u32[]{:S(2)}) copy-start(bf16[2048,256]{1,0:T(8,128)(2,1)} %wq_hbm.1) | copy-start | bytes 3145732
  0.9 1.9 %copy-start.1 = (bf16[256,2048]{1,0:T(8,128)(2,1)S(1)}, bf16[256,2048]{1,0:T(8,128)(2,1)}, u32[]{:S(2)}) copy-start(bf16[256,2048]{1,0:T(8,128)(2,1)} %wout_hbm.1) | copy-start | bytes 3145732
  2.4 0.7 copy-start.6
  2.4 0.7 copy-start.7
  2.4 0.7 copy-start.8

commit v3 on v2

v3 whole, which is shorter than its diff:
```python
import functools

import jax
import jax.numpy as jnp
from jax import lax
from jax.experimental import pallas as pl
from jax.experimental.pallas import tpu as pltpu
from jax.sharding import PartitionSpec as P

HD = 128
LEN = 4096
CORES = 2
PARTS = 2
NY = 8
F32, BF16, I32 = jnp.float32, jnp.bfloat16, jnp.int32
VMEM_LIMIT = 61 * 1024 * 1024


def rms(x, gain):
    return x * lax.rsqrt(jnp.mean(x * x, axis=-1, keepdims=True) + 1e-06) * gain


def iota(shape, dim):
    return lax.broadcasted_iota(I32, shape, dim)


def onehot(mask):
    return jnp.where(mask, 1.0, 0.0).astype(BF16)


def dot(a, b):
    return jnp.dot(a, b, preferred_element_type=F32)


def signal(sem, **where):
    pl.semaphore_signal(sem, inc=1, device_id=where, device_id_type=pl.DeviceIdType.MESH)


def remote(src, dst, send, recv, **where):
    return pltpu.make_async_remote_copy(
        src_ref=src, dst_ref=dst, send_sem=send, recv_sem=recv,
        device_id=where, device_id_type=pl.DeviceIdType.MESH,
    )


class ZRing:
    def __init__(self, piece, send, recv, n):
        self.piece, self.send, self.recv, self.n = piece, send, recv, n
        self.far = n // 2
        self.me = lax.axis_index("item")

    def copy(self, way, part, hop, shard):
        step = 1 if way == 0 else self.n - 1
        ref = self.piece(part, shard, way if hop == self.far else None)
        at = (way, part, hop - 1)
        return remote(
            ref, ref, self.send.at[at], self.recv.at[at], item=lax.rem(self.me + step, self.n)
        )

    def shard(self, way, hop):
        return lax.rem(self.me + (self.n - hop if way == 0 else hop), self.n)

    def start(self, part):
        for way in range(2):
            self.copy(way, part, 1, self.me).start()

    def land(self, part, hop):
        for way in range(2):
            self.copy(way, part, hop, self.shard(way, hop)).wait_recv()
            if hop < self.far:
                self.copy(way, part, hop + 1, self.shard(way, hop)).start()

    def drain(self, parts):
        for part in range(parts):
            for hop in range(1, self.far + 1):
                for way in range(2):
                    self.copy(way, part, hop, self.shard(way, hop - 1)).wait_send()


def rank_of(ids_row, ids_col, per_dev, n_seq, axis):
    rows = ids_row.shape[1]
    owner_row = (ids_row // per_dev) & (n_seq - 1)
    owner_col = (ids_col // per_dev) & (n_seq - 1)
    lane, sub = iota((rows, rows), 1), iota((rows, rows), 0)
    if axis == 0:
        same = (owner_col == owner_row) & (sub < lane)
        less = owner_col < owner_row
    else:
        same = (owner_col == owner_row) & (lane < sub)
        less = owner_row < owner_col
    within = jnp.sum(jnp.where(same, 1.0, 0.0), axis=axis, keepdims=True).astype(I32)
    before = jnp.sum(jnp.where(less, 1.0, 0.0), axis=axis, keepdims=True).astype(I32)
    return before + within, within


def kernel(
    n_item, n_seq, ny, len_ref, ids_hbm, states_hbm, igain_hbm, again_hbm, qg_hbm, kg_hbm,
    wq_hbm, wkv_hbm, wout_hbm, out_ref, ids_row_ref, states_ref, igain_ref, again_ref, qg_ref, kg_ref,
    wq_ref, wkv_raw, wkv_ref, wout_ref, table, id_a, id_b, id_c, id_d, wide, parcel, landed,
    every, order, query, kv, bias, acc, top, total, attn_ref, res_ref, outgo, income,
    w_sem, t_send, t_recv, iy_send, iy_recv, ix_send, ix_recv, row_send, row_recv,
    z_send, z_recv, lane_send, lane_recv, pair_send, pair_recv, o_send, o_recv,
):
    nq = n_seq // ny
    far = n_item // 2
    me = lax.axis_index("item")
    my_seq = lax.axis_index("seq")
    core = lax.rem(my_seq, CORES)
    other = 1 - core
    sibling = my_seq + 1 - 2 * core
    my_y = lax.rem(my_seq // CORES, ny)
    my_x = my_seq // (CORES * ny)
    my_q = my_x * CORES + core
    per_dev, width = states_ref.shape
    rows = ids_row_ref.shape[1]
    share = rows // n_item
    span = LEN // rows
    chips = span // CORES
    chip = lax.rem(my_seq // CORES, chips)
    not_last = chip < chips - 1
    base = lax.rem(my_seq, span) * rows
    length = len_ref[my_seq // span]
    q_cols = wq_ref.shape[1]
    group = q_cols // HD
    out_cols = width // n_item
    parts = every.shape[0]
    cols = width // parts

    def along_y(y):
        return (my_x * ny + y) * CORES + core

    def along_q(q):
        return ((q // CORES) * ny + my_y) * CORES + lax.rem(q, CORES)

    def y_plus(d):
        return lax.rem(my_y + d, ny)

    def q_plus(d):
        return lax.rem(my_q + d, nq)

    n_mate = nq * ny
    my_mate = my_q * ny + my_y

    def mate_seq(m):
        q, y = m // ny, lax.rem(m, ny)
        return ((q // CORES) * ny + y) * CORES + lax.rem(q, CORES)

    def to_mates(do):
        def one(d, _):
            do(lax.rem(my_mate + d, n_mate))
            do(lax.rem(my_mate + n_mate - d, n_mate))
            return 0

        lax.fori_loop(1, n_mate // 2, one, 0)
        do(lax.rem(my_mate + n_mate // 2, n_mate))

    barrier = pltpu.get_barrier_semaphore()
    for step in (1, n_item - 1):
        signal(barrier, item=lax.rem(me + step, n_item))
    to_mates(lambda m: signal(barrier, seq=mate_seq(m)))

    small = [(states_hbm, states_ref), (igain_hbm, igain_ref), (ids_hbm, ids_row_ref)]
    large = [(again_hbm, again_ref), (qg_hbm, qg_ref), (kg_hbm, kg_ref)]
    large += [(wq_hbm, wq_ref), (wkv_hbm, wkv_raw), (wout_hbm, wout_ref)]
    small, large = (
        [pltpu.make_async_copy(a, b, w_sem.at[at + i]) for i, (a, b) in enumerate(pairs)]
        for at, pairs in ((0, small), (len(small), large))
    )
    for copy in small + large:
        copy.start()
    for copy in small:
        copy.wait()

    embed = rms(states_ref[...].astype(F32), igain_ref[...]).astype(BF16)
    for part in range(parts):
        table[part, me] = embed[:, part * cols:(part + 1) * cols]
    pl.semaphore_wait(barrier, 2 + n_mate - 1)

    def table_piece(part, shard, way):
        if way is None:
            return table.at[part, shard]
        return table.at[part, shard, pl.ds(way * (per_dev // 2), per_dev // 2)]

    items_ring = ZRing(table_piece, t_send, t_recv, n_item)
    for part in range(parts):
        items_ring.start(part)

    def land_items(hop):
        for part in range(parts):
            items_ring.land(part, hop)

    ids_row = ids_row_ref[...]
    diagonal = iota((rows, rows), 0) == iota((rows, rows), 1)
    ids_col = jnp.sum(jnp.where(diagonal, ids_row.astype(F32), 0.0), axis=1, keepdims=True).astype(I32)
    rank, within = rank_of(ids_row, ids_col, per_dev, n_seq, 0)
    owner = ids_row // per_dev
    owner_seq = owner & (n_seq - 1)
    source_y = (owner_seq // CORES) & (ny - 1)
    source_q = (owner_seq // (CORES * ny)) * CORES + (owner_seq & (CORES - 1))
    item = (owner // n_seq) * per_dev + (ids_row & (per_dev - 1)) + 1
    asks_at = rank & (n_item - 1)
    asks = asks_at == me
    copy_no = within // n_item
    place = jnp.where(asks, source_y * nq + source_q, -1)
    asked = []
    for sub in range(2):
        hit = (iota((ny * nq, rows), 0) == place) & (copy_no == sub)
        asked.append(jnp.sum(jnp.where(hit, item.astype(F32), 0.0), axis=1, keepdims=True).astype(I32))
    lanes = iota((ny * nq, 128), 1)
    id_a[...] = jnp.where(lanes == 0, asked[0], jnp.where(lanes == 1, asked[1], 0)).reshape(ny, nq, 128)

    def ids_y(d, y_from, y_to):
        return remote(
            id_a.at[y_to], id_b.at[y_from], iy_send.at[d - 1], iy_recv.at[d - 1], seq=along_y(y_to)
        )

    def ids_q(d, q_from, q_to):
        return remote(
            id_c.at[q_to], id_d.at[q_from], ix_send.at[d - 1], ix_recv.at[d - 1], seq=along_q(q_to)
        )

    for d in range(1, ny):
        ids_y(d, my_y, y_plus(d)).start()
    id_b[my_y] = id_a[my_y]

    spot = jnp.where(asks, rank // n_item, -1)
    pick_a = onehot(iota((share, rows), 0) == spot)
    sent = jnp.where(asks, copy_no * n_mate + source_q * ny + source_y, -1)
    pick_b = onehot(iota((2 * n_mate, rows), 0) == sent)
    pick = lax.dot_general(pick_a, pick_b, (((1,), (1,)), ((), ())), preferred_element_type=F32).astype(BF16)

    for d in range(1, ny):
        ids_y(d, y_plus(ny - d), my_y).wait_recv()
    for q in range(nq):
        id_c[q] = id_b[:, q, :]
    for d in range(1, nq):
        ids_q(d, my_q, q_plus(d)).start()
    id_d[my_q] = id_c[my_q]
    land_items(1)

    def landing(rank):
        apart = (rank - me + n_item) & (n_item - 1)
        place = jnp.where(apart == 0, 0, jnp.where(apart < far, 2 * apart, 2 * (n_item - apart) - 1))
        return place * share + rank // n_item

    goal_row = asks_at * share + rank // n_item
    pos_col = jnp.sum(
        jnp.where(goal_row == iota((rows, rows), 0), iota((rows, rows), 1).astype(F32), 0.0), axis=1, keepdims=True
    ).astype(I32)
    rank_col, _ = rank_of(ids_row, ids_col, per_dev, n_seq, 1)
    order[...] = onehot((rank_col & (n_item - 1)) * share + rank_col // n_item == iota((rows, rows), 1))
    placed = landing(rank_col) == iota((rows, rows), 1)
    pos_row = jnp.sum(jnp.where(placed, iota((rows, rows), 0).astype(F32), 0.0), axis=0, keepdims=True).astype(I32)
    bias[core] = jnp.broadcast_to(jnp.where(base + pos_row < length, 0.0, -jnp.inf), (8, rows))
    if far > 2:
        land_items(2)

    chunks = [slice(0, 3 * share if far > 1 else 2 * share)]
    for hop in range(2, far + 1):
        chunks.append(slice((2 * hop - 1) * share, min(2 * hop + 1, n_item) * share))
    n_chunks = len(chunks)

    def block(slot, c):
        if c < 0:
            return bias.at[slot]
        return kv.at[slot, pl.ds(chunks[c].start, chunks[c].stop - chunks[c].start)]

    def lane_copy(hop, c, far_off=False):
        return remote(
            block(core if far_off else (hop - 1) * 2 + core, c), block(hop * 2 + core, c),
            lane_send.at[hop - 1, c + 1], lane_recv.at[hop - 1, c + 1],
            seq=my_seq + (hop if far_off else 1) * CORES,
        )

    def pair_copy(hop, c, lane):
        return remote(
            block(hop * 2 + lane, c), block(hop * 2 + lane, c),
            pair_send.at[hop, c + 1], pair_recv.at[hop, c + 1], seq=sibling,
        )

    straight = range(n_chunks - 1, n_chunks)

    def give(c):
        if c in straight:
            for hop in range(1, chips):
                @pl.when(chip + hop < chips)
                def _():
                    lane_copy(hop, c, True).start()
        else:
            @pl.when(not_last)
            def _():
                lane_copy(1, c).start()

        @pl.when(core == 0)
        def _():
            pair_copy(0, c, 0).start()

    def take(hop, c):
        @pl.when(chip >= hop)
        def _():
            lane_copy(hop, c).wait_recv()
            if hop < chips - 1 and c not in straight:
                @pl.when(not_last)
                def _():
                    lane_copy(hop + 1, c).start()
            pair_copy(hop, c, core).start()

    def pass_on(stage):
        for hop in range(1, chips):
            for c in range(-1, n_chunks):
                if c not in straight and 2 * (c + 1) + hop == stage:
                    take(hop, c)

    give(-1)
    for hop in range(3, far):
        land_items(hop)
    for copy in large:
        copy.wait()
    strip = min(128, width)
    to, frm = iota((2 * strip, 2 * strip), 0), iota((2 * strip, 2 * strip), 1)
    split = onehot(frm == lax.rem(to, strip) * 2 + to // strip)
    for first in range(0, width, strip):
        both = dot(split, wkv_raw[first * 2:(first + strip) * 2]).astype(BF16)
        wkv_ref[first:first + strip, :HD] = both[:strip]
        wkv_ref[first:first + strip, HD:] = both[strip:]

    for d in range(1, nq):
        ids_q(d, q_plus(nq - d), my_q).wait_recv()
    wanted = id_d[...].reshape(nq * ny, 128)
    names = iota((nq * ny, n_item * per_dev), 1) + 1
    choose = [onehot(wanted[:, sub:sub + 1] == names) for sub in range(2)]
    blocks = width // HD
    tall = 2 * blocks

    def rows_copy(m_from, m_to):
        return remote(
            parcel.at[m_to], landed.at[m_from], row_send.at[0], row_recv.at[0], seq=mate_seq(m_to)
        )

    def all_but_one(buf, sem):
        ref = buf.at[pl.ds(0, n_mate - 1)]
        return pltpu.make_async_copy(ref, ref, sem.at[0])

    def rows_piece(part, shard, way):
        if way is None:
            return every.at[part, shard]
        return every.at[part, shard, pl.ds(way * (share // 2), share // 2)]

    ring = ZRing(rows_piece, z_send, z_recv, n_item)

    for part in range(parts):
        if far > 1:
            items_ring.land(part, far)
        source = table[part].reshape(n_item * per_dev, cols)
        for sub in range(2):
            picked = dot(choose[sub], source)
            for k in range(cols // HD):
                at = sub * blocks + part * (cols // HD) + k
                wide[pl.ds(at, n_mate, stride=tall), :] = picked[:, k * HD:(k + 1) * HD]
    parcel[...] = wide[...].reshape(n_mate, tall, HD).astype(BF16)
    to_mates(lambda m: rows_copy(my_mate, m).start())
    landed[my_mate] = parcel[my_mate]

    all_but_one(landed, row_recv).wait()
    wide[...] = landed[...].reshape(n_mate * tall, HD).astype(F32)
    for part in range(parts):
        for k in range(cols // HD):
            at = part * (cols // HD) + k
            came = jnp.concatenate(
                [wide[pl.ds(sub * blocks + at, n_mate, stride=tall), :] for sub in range(2)], axis=0
            ).astype(BF16)
            every[part, me, :, k * HD:(k + 1) * HD] = dot(pick, came).astype(BF16)
        ring.start(part)

    scale = 1.4426950408889634 / HD**0.5

    def project(hop):
        shards = [me] if hop == 0 else [ring.shard(0, hop)] + ([ring.shard(1, hop)] if hop < far else [])
        first = 0 if hop == 0 else (2 * hop - 1) * share
        here = slice(first, first + len(shards) * share)
        x = jnp.concatenate(
            [jnp.concatenate([every[part, j] for part in range(parts)], axis=1) for j in shards], axis=0
        )
        normed = rms(x.astype(F32), again_ref[...]).astype(BF16)
        q = dot(normed, wq_ref[...])
        key = dot(normed, wkv_ref[:, :HD])
        value = dot(normed, wkv_ref[:, HD:])
        for g in range(group):
            piece = rms(q[:, g * HD:(g + 1) * HD], qg_ref[...] * scale).astype(BF16)
            for at, j in enumerate(shards):
                there = pl.ds(pl.multiple_of(g * rows + j * share, share), share)
                query[there] = piece[at * share:(at + 1) * share]
        kv[core, here, :HD] = rms(key, kg_ref[...]).astype(BF16)
        kv[core, here, HD:] = value.astype(BF16)

    project(0)
    for hop in range(1, far + 1):
        ring.land(0, hop)
        pass_on(2 * hop - 1)
        ring.land(1, hop)
        project(hop)
        give(hop - 1)
        pass_on(2 * hop)

    def spread(x):
        return x[:, :rows] if rows < HD else jnp.concatenate([x] * (rows // HD), axis=1)

    def absorb(blocks, first):
        for g in range(group):
            here = slice(g * rows, (g + 1) * rows)
            q = query[here]
            if first:
                old = jnp.full((rows, HD), -1e30, F32)
            else:
                old, whole, out = top[here], total[here], acc[here]
            for slot in blocks:
                score = lax.dot_general(
                    q, kv[slot, :, :HD], (((1,), (1,)), ((), ())), preferred_element_type=F32
                ) + bias[slot, 0:1]
                if first:
                    score = jnp.where(pos_row <= pos_col, score, -jnp.inf)
                new = jnp.maximum(old, jnp.max(score, axis=-1, keepdims=True))
                weights = jnp.exp2(score - spread(new))
                part = jnp.sum(weights, axis=-1, keepdims=True)
                more = dot(weights.astype(BF16), kv[slot, :, HD:])
                if first:
                    whole, out = jnp.broadcast_to(part, (rows, HD)), more
                else:
                    shrink = jnp.exp2(old - new)
                    whole, out = whole * shrink + part, out * shrink + more
                old = new
            top[here], total[here], acc[here] = old, whole, out

    absorb([core], True)
    pass_on(2 * far + 1)
    take(1, straight[0])

    @pl.when(core == 1)
    def _():
        for c in range(-1, n_chunks):
            pair_copy(0, c, 0).wait_recv()
        absorb([0], False)

    for stage in range(2 * far + 2, 2 * far + chips):
        pass_on(stage)
    for hop in range(2, chips):
        take(hop, straight[0])
    for last in range(1, chips):
        @pl.when(chip == last)
        def _():
            for hop in range(1, last + 1):
                for c in range(-1, n_chunks):
                    pair_copy(hop, c, other).wait_recv()
            absorb([2 * hop + lane for hop in range(1, last + 1) for lane in range(2)], False)

    seen = jnp.concatenate(
        [(acc[g * rows:(g + 1) * rows] / total[g * rows:(g + 1) * rows]).astype(BF16) for g in range(group)], axis=1
    )
    fine = base + pos_col < length
    attn_ref[...] = jnp.where(fine, seen, jnp.zeros_like(seen))

    half_rows = rows // 2
    plan = []
    for way in range(2):
        steps = [(far, way)]
        for k in range(far - 1, 0, -1):
            steps += [(k, 1 - way), (k, way)]
        plan.append(steps)

    def partial(goal, half):
        here = pl.ds(pl.multiple_of(goal * out_cols, out_cols), out_cols)
        return dot(attn_ref[half * half_rows:(half + 1) * half_rows], wout_ref[:, here])

    def sum_copy(way, at):
        step = 1 if way == 0 else n_item - 1
        return remote(
            outgo.at[way, at], income.at[way, at], o_send.at[way, at], o_recv.at[way, at],
            item=lax.rem(me + step, n_item),
        )

    for at in range(len(plan[0])):
        for way in range(2):
            k, half = plan[way][at]
            goal = lax.rem(me + (k if way == 0 else n_item - k), n_item)
            value = partial(goal, half)
            if (k + 1, half) in plan[way]:
                before = plan[way].index((k + 1, half))
                sum_copy(way, before).wait_recv()
                value = value + income[way, before].astype(F32)
            outgo[way, at] = value.astype(BF16)
            sum_copy(way, at).start()
    where = me * out_cols
    inside = pl.ds(pl.multiple_of(lax.rem(where, cols), out_cols), out_cols)
    for half in (1, 0):
        here = slice(half * half_rows, (half + 1) * half_rows)
        first = half * (n_item // 2)
        own = every[where // cols, first:first + n_item // 2, :, inside].reshape(half_rows, out_cols)
        value = partial(me, half) + own.astype(F32)
        for way in range(2):
            if (1, half) in plan[way]:
                at = plan[way].index((1, half))
                sum_copy(way, at).wait_recv()
                value = value + income[way, at].astype(F32)
        res_ref[here] = value.astype(BF16)
    out_ref[...] = dot(order[...], res_ref[...]).astype(BF16)

    items_ring.drain(parts)
    ring.drain(parts)
    for d in range(1, ny):
        ids_y(d, my_y, y_plus(d)).wait_send()
    for d in range(1, nq):
        ids_q(d, my_q, q_plus(d)).wait_send()
    all_but_one(parcel, row_send).wait()
    for c in range(-1, n_chunks):
        @pl.when(core == 0)
        def _():
            pair_copy(0, c, 0).wait_send()

        for hop in range(1, chips):
            if c in straight:
                @pl.when(chip + hop < chips)
                def _():
                    lane_copy(hop, c, True).wait_send()
            else:
                @pl.when((chip >= hop - 1) & not_last)
                def _():
                    lane_copy(hop, c).wait_send()

            @pl.when(chip >= hop)
            def _():
                pair_copy(hop, c, core).wait_send()

    for way in range(2):
        for at in range(len(plan[0])):
            sum_copy(way, at).wait_send()


def body(ny, item_states, item_gain, hist_ids, lengths, attn_gain, w_q, w_kv, q_gain, k_gain, w_out):
    n_seq = lax.axis_size("seq")
    n_item = lax.axis_size("item")
    nq = n_seq // ny
    per_dev, width = item_states.shape
    rows = hist_ids.shape[0]
    share = rows // n_item
    far = n_item // 2
    span = LEN // rows
    chips = span // CORES
    out_cols = width // n_item
    q_cols = w_q.shape[1]
    group = q_cols // HD
    cols = width // PARTS
    tall = 2 * width // HD
    steps = 2 * far - 1
    dma = pltpu.SemaphoreType.DMA
    vmem, smem, hbm = (pl.BlockSpec(memory_space=space) for space in (pltpu.VMEM, pltpu.SMEM, pl.ANY))
    return pl.pallas_call(
        functools.partial(kernel, n_item, n_seq, ny),
        out_shape=jax.ShapeDtypeStruct((rows, out_cols), BF16),
        in_specs=[smem] + [hbm] * 9,
        out_specs=vmem,
        scratch_shapes=[
            pltpu.VMEM((1, rows), I32),
            pltpu.VMEM((per_dev, width), BF16),
            pltpu.VMEM((1, width), F32),
            pltpu.VMEM((1, width), F32),
            pltpu.VMEM((1, HD), F32),
            pltpu.VMEM((1, HD), F32),
            pltpu.VMEM((width, q_cols), BF16),
            pltpu.VMEM((width * 2, HD), BF16),
            pltpu.VMEM((width, 2 * HD), BF16),
            pltpu.VMEM((q_cols, width), BF16),
            pltpu.VMEM((PARTS, n_item, per_dev, cols), BF16),
            pltpu.VMEM((ny, nq, 128), I32),
            pltpu.VMEM((ny, nq, 128), I32),
            pltpu.VMEM((nq, ny, 128), I32),
            pltpu.VMEM((nq, ny, 128), I32),
            pltpu.VMEM((n_seq * tall, HD), F32),
            pltpu.VMEM((n_seq, tall, HD), BF16),
            pltpu.VMEM((n_seq, tall, HD), BF16),
            pltpu.VMEM((PARTS, n_item, share, cols), BF16),
            pltpu.VMEM((rows, rows), BF16),
            pltpu.VMEM((group * rows, HD), BF16),
            pltpu.VMEM((span, rows, 2 * HD), BF16),
            pltpu.VMEM((span, 8, rows), F32),
            pltpu.VMEM((group * rows, HD), F32),
            pltpu.VMEM((group * rows, HD), F32),
            pltpu.VMEM((group * rows, HD), F32),
            pltpu.VMEM((rows, q_cols), BF16),
            pltpu.VMEM((rows, out_cols), BF16),
            pltpu.VMEM((2, steps, rows // 2, out_cols), BF16),
            pltpu.VMEM((2, steps, rows // 2, out_cols), BF16),
            dma((9,)),
            dma((2, PARTS, far)), dma((2, PARTS, far)),
            dma((ny,)), dma((ny,)), dma((nq,)), dma((nq,)),
            dma((1,)), dma((1,)),
            dma((2, PARTS, far)), dma((2, PARTS, far)),
            dma((chips - 1, far + 1)), dma((chips - 1, far + 1)),
            dma((chips, far + 1)), dma((chips, far + 1)),
            dma((2, steps)), dma((2, steps)),
        ],
        compiler_params=pltpu.CompilerParams(
            collective_id=1, has_side_effects=True, vmem_limit_bytes=VMEM_LIMIT
        ),
        name="user_layer",
    )(
        lengths, hist_ids.reshape(1, rows), item_states,
        item_gain.reshape(1, width), attn_gain.reshape(1, width), q_gain.reshape(1, HD),
        k_gain.reshape(1, HD), w_q, w_kv.reshape(width * 2, HD), w_out,
    )


def solution(mesh):
    placed = (
        P(("item", "seq"), None),
        P(),
        P("seq"),
        P(),
        P(),
        P(None, "item"),
        P(None, None, "item"),
        P(),
        P(),
        P("item", None),
    )
    return jax.shard_map(
        functools.partial(body, NY),
        mesh=mesh, in_specs=placed, out_specs=P("seq", "item"), check_vma=False,
    )
```

time: 126 us -> 110 us (0.87); the launches traced: 124 us -> 110 us
  Pallas kernels: 121 us -> 108 us
  local copies, waits for them, and re-layouts: 3.76 us -> 1.67 us
    pallas_call x1, Pallas kernels: 121 us -> 108 us  [body(): pl.pallas_call(functools.partial(kernel, n_item, n_seq, ny), out_shape=ja...]
    unnamed x20 -> x1, local copies, waits for them, and re-layouts: 3.62 us -> 1.67 us
where the time goes in v3:
time: 110 us
  Pallas kernels  108 us (98%)
  local copies, waits for them, and re-layouts  1.67 us (2%)
    pallas_call x1, Pallas kernels, body(): pl.pallas_call(functools.partial(kernel, n_item, n_seq, ny), out_shape=ja...  108 us

profile of v3, /device:TPU:56, one launch (start us, length us, event | category | flops | bytes accessed | tf_op | source)
XLA Modules:
  0.0 109.9 jit_solution(15051632808408738959)
XLA Ops:
  0.0 108.2 %user_layer.1 = bf16[512,256]{1,0:T(8,128)(2,1)} custom-call(s32[8]{0:T(128)} %len_ref.1, s32[1,512]{1,0:T(1,128)} %bitcast.9, bf16[32,2048]{1,0:T(8,128)(2,1)} %states_hbm.1, f32[1,2048]{1,0:T(1,128)} %bitcast.7, f32[1,2048]{1,0:T(1,128)} %bitcast.8, f32[1,128]{1,0:T(1,128)} %bitcast.10, f32[1,128]{1,0:T(1,128)} %bitcast.11, bf16[2048,256]{1,0:T(8,128)(2,1)} %wq_hbm.1, ...), custom_call_target="tpu_custom_call" | custom-call | tf_op jit(solution)/shard_map/user_layer/pallas_call | solution.py:556
  108.2 1.7 %copy.12 = bf16[512,256]{1,0:T(8,128)(2,1)} copy(bf16[512,256]{1,0:T(8,128)(2,1)} %user_layer.1) | data formatting | bytes 524288

commit v4 on v3

--- a/solution.py
+++ b/solution.py
@@ -154,11 +154,6 @@
         lax.fori_loop(1, n_mate // 2, one, 0)
         do(lax.rem(my_mate + n_mate // 2, n_mate))
 
-    barrier = pltpu.get_barrier_semaphore()
-    for step in (1, n_item - 1):
-        signal(barrier, item=lax.rem(me + step, n_item))
-    to_mates(lambda m: signal(barrier, seq=mate_seq(m)))
-
     small = [(states_hbm, states_ref), (igain_hbm, igain_ref), (ids_hbm, ids_row_ref)]
     large = [(again_hbm, again_ref), (qg_hbm, qg_ref), (kg_hbm, kg_ref)]
     large += [(wq_hbm, wq_ref), (wkv_hbm, wkv_raw), (wout_hbm, wout_ref)]
@@ -168,6 +163,12 @@
     )
     for copy in small + large:
         copy.start()
+
+    barrier = pltpu.get_barrier_semaphore()
+    for step in (1, n_item - 1):
+        signal(barrier, item=lax.rem(me + step, n_item))
+    to_mates(lambda m: signal(barrier, seq=mate_seq(m)))
+
     for copy in small:
         copy.wait()
 

time: 110 us -> 110 us (level)
  no operation moved by 1% of the time
where the time goes in v4:
time: 110 us
  Pallas kernels  108 us (98%)
  local copies, waits for them, and re-layouts  1.67 us (2%)
    pallas_call x1, Pallas kernels, body(): pl.pallas_call(functools.partial(kernel, n_item, n_seq, ny), out_shape=ja...  108 us

profile of v4, /device:TPU:56, one launch (start us, length us, event | category | flops | bytes accessed | tf_op | source)
XLA Modules:
  0.0 109.7 jit_solution(20683722150755285)
XLA Ops:
  0.0 108.0 %user_layer.1 = bf16[512,256]{1,0:T(8,128)(2,1)} custom-call(s32[8]{0:T(128)} %len_ref.1, s32[1,512]{1,0:T(1,128)} %bitcast.9, bf16[32,2048]{1,0:T(8,128)(2,1)} %states_hbm.1, f32[1,2048]{1,0:T(1,128)} %bitcast.7, f32[1,2048]{1,0:T(1,128)} %bitcast.8, f32[1,128]{1,0:T(1,128)} %bitcast.10, f32[1,128]{1,0:T(1,128)} %bitcast.11, bf16[2048,256]{1,0:T(8,128)(2,1)} %wq_hbm.1, ...), custom_call_target="tpu_custom_call" | custom-call | tf_op jit(solution)/shard_map/user_layer/pallas_call | solution.py:557
  108.0 1.7 %copy.12 = bf16[512,256]{1,0:T(8,128)(2,1)} copy(bf16[512,256]{1,0:T(8,128)(2,1)} %user_layer.1) | data formatting | bytes 524288
